TPU v7x, 32 devices: a whole 2x2x4 slice. The times are simulated.
32 devices in a mesh: section: 2 (over x), gx: 4 (over y, core), gy: 4 (over z).
Axes of the slice: x: 2, y: 2, z: 4, core: 2. Of those that a mesh axis runs over, the one named last changes fastest.
Arguments:
- hidden_in: bfloat16 [4096, 2048], P('gx', 'gy'), may hold values from -6 to 6
- out_grad: bfloat16 [4096, 2048], P('gx', 'gy'), may hold values from -6 to 6
- lengths: int32 [4], replicated, may hold values from 512 to 1024, as said below
- dealing: int32 [4], replicated, may hold values from 0 to 3, each once
- attn_gain: bfloat16 [2, 2048], P('section', 'gx'), may hold values from 0.25 to 1.75
- w_query: bfloat16 [2, 2048, 2048], P('section', 'gx', 'gy'), may hold values from -0.125 to 0.125
- w_key: bfloat16 [2, 2048, 256], P('section', 'gx'), may hold values from -0.125 to 0.125
- w_value: bfloat16 [2, 2048, 256], P('section', 'gx'), may hold values from -0.125 to 0.125
- w_out: bfloat16 [2, 2048, 2048], P('section', 'gy', 'gx'), may hold values from -2 to 2
- mlp_gain: bfloat16 [2, 2048], P('section', 'gx'), may hold values from 0.25 to 1.75
- w_gate: bfloat16 [2, 2048, 5632], P('section', 'gx', 'gy'), may hold values from -0.125 to 0.125
- w_up: bfloat16 [2, 2048, 5632], P('section', 'gx', 'gy'), may hold values from -0.125 to 0.125
- w_down: bfloat16 [2, 5632, 2048], P('section', 'gy', 'gx'), may hold values from -0.078125 to 0.078125
Outputs:
- layer_outputs: bfloat16 [2, 4096, 2048], P('section', 'gx', 'gy')
- norm_rms: float32 [2, 2, 4096], P('section', None, 'gx')
- input_grads: bfloat16 [2, 4096, 2048], P('section', 'gx', 'gy')
- attn_gain_grad: float32 [2, 2048], P('section', 'gx')
- query_grad: float32 [2, 2048, 2048], P('section', 'gx', 'gy')
- key_grad: float32 [2, 2048, 256], P('section', 'gx')
- value_grad: float32 [2, 2048, 256], P('section', 'gx')
- out_proj_grad: float32 [2, 2048, 2048], P('section', 'gy', 'gx')
- mlp_gain_grad: float32 [2, 2048], P('section', 'gx')
- gate_grad: float32 [2, 2048, 5632], P('section', 'gx', 'gy')
- up_grad: float32 [2, 2048, 5632], P('section', 'gx', 'gy')
- down_grad: float32 [2, 5632, 2048], P('section', 'gy', 'gx')
Inputs may be any that keep to these rules, and one draw needn't show every extreme that they name: `lengths`: one sequence has exactly 1024 tokens and one exactly 512. `dealing`: a permutation of the token shards.
All inputs are finite; a program needn't handle non-finite values.
Results may differ from a plain program's by a relative error of at most 0.04.
Values may be sent and summed in bfloat16 or wider, within the bound.
A program may use at most 320 MiB of HBM per device.

v0:
```python
import functools

import jax
import jax.numpy as jnp
from jax import lax
from jax.experimental import pallas as pl
from jax.experimental.pallas import tpu as pltpu
from jax.sharding import PartitionSpec as P

QH = 32
KVH = 4
HD = 64
LAYERS = 2
EPS = 1e-05
BF = jnp.bfloat16
F32 = jnp.float32
MESH = pl.DeviceIdType.MESH
CHUNK = 32
STEPS = 2
GAIN_ROWS = 32
VMEM_LIMIT = 56 * 1024 * 1024
ANY = pl.BlockSpec(memory_space=pl.ANY)
VMEM = pl.BlockSpec(memory_space=pltpu.VMEM)


def mm(left, right, dims=((1,), (0,))):
    return lax.dot_general(left, right, (dims, ((), ())), preferred_element_type=F32)


def swap_pairs(values, axis, by=1):
    count = lax.axis_size(axis)
    return lax.ppermute(values, axis, [(i, i ^ by) for i in range(count)])


def rope_tables(places):
    half_width = HD // 2
    frequency = jnp.power(10000.0, -2.0 * jnp.arange(half_width).astype(F32) / HD)
    angles = frequency[:, None] * places.astype(F32)[None, :]
    return jnp.cos(angles), jnp.sin(angles)


def core_rows(rows, core):
    quarter = rows.shape[0] // 4
    low = lax.dynamic_slice_in_dim(rows, core * quarter, quarter, 0)
    high = lax.dynamic_slice_in_dim(rows, (3 - core) * quarter, quarter, 0)
    return jnp.concatenate([low, high], axis=0)


def join_halves(first, second):
    quarter = first.shape[0] // 2
    return jnp.concatenate(
        [first[:quarter], second[:quarter], second[quarter:], first[quarter:]], axis=0
    )


def chip_groups():
    return [[0, 2], [1, 3]]


def gather_blocks(base):
    return lax.all_gather(base, "gx", axis=0)


def chosen(pair, layer):
    return jnp.where(lax.axis_index("section") == layer, *pair)


def with_own(stack, pair, layer):
    shard = lax.axis_index("gx")
    return lax.dynamic_update_index_in_dim(stack, chosen(pair, layer), shard, 0)


def fused():
    return lax.axis_size("gx") == 4 and lax.axis_size("gy") == 4


def tall(w):
    return w.reshape(-1, w.shape[-1])


def side(w):
    return jnp.concatenate([w[i] for i in range(w.shape[0])], axis=1)


def cut(w, low, high):
    return w[:, :-GAIN_ROWS, low:high]


def shard_sum(product):
    return lax.psum_scatter(product, "gx", scatter_dimension=0, tiled=True)


def chip_sum(product):
    product = product.reshape(-1, product.shape[-1])
    return lax.psum_scatter(
        product, "gx", scatter_dimension=0, tiled=True, axis_index_groups=[[0, 2], [1, 3]]
    )


def line_gather_kernel(mine_ref, out_ref, right_send, right_recv, left_send, left_recv):
    z = lax.axis_index("gy")
    rows, columns = mine_ref.shape
    half = rows // 2
    barrier = pltpu.get_barrier_semaphore()
    for near, there in ((z - 1, z > 0), (z + 1, z < 3)):

        @pl.when(there)
        def _():
            pl.semaphore_signal(barrier, inc=1, device_id={"gy": near}, device_id_type=MESH)

    inner = (z > 0) & (z < 3)
    pl.when(inner)(lambda: pl.semaphore_wait(barrier, 2))
    pl.when(jnp.logical_not(inner))(lambda: pl.semaphore_wait(barrier, 1))

    def block(of):
        of = jnp.clip(of, 0, 3)
        return pl.ds(pl.multiple_of(of * columns, columns), columns)

    out_ref[:, block(z)] = mine_ref[...]

    def copy(step, p, right):
        here = out_ref.at[p * half : (p + 1) * half, block(z - step if right else z + step)]
        send, recv = (right_send, right_recv) if right else (left_send, left_recv)
        return pltpu.make_async_remote_copy(
            src_ref=here, dst_ref=here, send_sem=send.at[2 * step + p],
            recv_sem=recv.at[2 * step + p], device_id={"gy": z + 1 if right else z - 1},
            device_id_type=MESH,
        )

    right_at = [(z < 3) & (z >= step) for step in range(3)]
    left_at = [(z > 0) & (z <= 3 - step) for step in range(3)]
    for step in range(4):
        for p in range(2):
            if step > 0:
                pl.when(z >= step)(lambda: copy(step - 1, p, True).wait_recv())
                pl.when(z <= 3 - step)(lambda: copy(step - 1, p, False).wait_recv())
            if step < 3:
                pl.when(right_at[step])(lambda: copy(step, p, True).start())
                pl.when(left_at[step])(lambda: copy(step, p, False).start())
    for step in range(3):
        for p in range(2):
            pl.when(right_at[step])(lambda: copy(step, p, True).wait_send())
            pl.when(left_at[step])(lambda: copy(step, p, False).wait_send())


def line_gather(mine):
    if not fused():
        return lax.all_gather(mine, "gy", axis=1, tiled=True)
    rows, columns = mine.shape
    dma = pltpu.SemaphoreType.DMA
    return pl.pallas_call(
        line_gather_kernel,
        out_shape=jax.ShapeDtypeStruct((rows, 4 * columns), BF),
        in_specs=[VMEM],
        out_specs=VMEM,
        scratch_shapes=[dma((6,))] * 4,
        compiler_params=pltpu.CompilerParams(
            collective_id=12, has_side_effects=True, vmem_limit_bytes=VMEM_LIMIT
        ),
        cost_estimate=pl.CostEstimate(flops=0, bytes_accessed=150_000_000, transcendentals=0),
        name="line_gather",
    )(mine)


def rope_down(values, cosine, sines):
    half_width = HD // 2
    first, second = values[:half_width], values[half_width:]
    return jnp.concatenate(
        [first * cosine - second * sines, second * cosine + first * sines], axis=0
    )


def fill_bias(bias_ref, key_ref, query_ref, length_ref):
    keys = key_ref[...]
    allowed = (keys <= query_ref[...]) & (keys < length_ref[...])
    bias_ref[...] = jnp.where(allowed, 0.0, -1e30)


def dot_to(left, right, dims):
    return lax.dot_general(left, right, (dims, ((), ())), preferred_element_type=F32)


def attend_kernel(
    q_ref, k_ref, vt_ref, cos_ref, sin_ref, key_ref, query_ref, length_ref,
    heads_ref, rot_ref, lse_ref, bias_ref, out_ref,
):
    fill_bias(bias_ref, key_ref, query_ref, length_ref)

    def head(h, carry):
        here = pl.ds(pl.multiple_of(h * HD, HD), HD)
        rotated = rope_down(q_ref[here, :], cos_ref[...], sin_ref[...]).astype(BF)
        rot_ref[here, :] = rotated
        scaled = (rotated.astype(F32) * HD ** (-0.5)).astype(BF)
        scores = dot_to(k_ref[...], scaled, ((1,), (0,))) + bias_ref[...]
        top = jnp.max(scores, axis=0, keepdims=True)
        exponent = jnp.exp(scores - top)
        total = jnp.sum(exponent, axis=0, keepdims=True)
        probs = (exponent * (1.0 / total)).astype(BF)
        out_ref[here, :] = dot_to(vt_ref[...], probs, ((1,), (0,)))
        lse_ref[pl.ds(h, 1), :] = top + jnp.log(total)
        return carry

    lax.fori_loop(0, q_ref.shape[0] // HD, head, 0)
    heads_ref[...] = out_ref[...].T.astype(BF)


def attend_back_kernel(
    rot_ref, k_ref, kt_ref, v_ref, d_ref, lse_ref, cos_ref, sin_ref, key_ref, query_ref, length_ref,
    dq_ref, dk_ref, dv_ref, bias_ref, out_ref,
):
    fill_bias(bias_ref, key_ref, query_ref, length_ref)
    dk_ref[...] = jnp.zeros_like(dk_ref)
    dv_ref[...] = jnp.zeros_like(dv_ref)
    scaling = HD ** (-0.5)

    def head(h, carry):
        here = pl.ds(pl.multiple_of(h * HD, HD), HD)
        scaled = (rot_ref[here, :].astype(F32) * scaling).astype(BF)
        scores = dot_to(k_ref[...], scaled, ((1,), (0,))) + bias_ref[...]
        probs = jnp.exp(scores - lse_ref[pl.ds(h, 1), :])
        d_probs = dot_to(v_ref[...], d_ref[here, :], ((1,), (0,)))
        delta = jnp.sum(probs * d_probs, axis=0, keepdims=True)
        d_scores = (probs * (d_probs - delta)).astype(BF)
        dk_ref[...] += dot_to(d_scores, scaled, ((1,), (1,)))
        dv_ref[...] += dot_to(probs.astype(BF), d_ref[here, :], ((1,), (1,)))
        dq = dot_to(kt_ref[...], d_scores, ((1,), (0,))) * scaling
        out_ref[here, :] = rope_down(dq, cos_ref[...], -sin_ref[...])
        return carry

    lax.fori_loop(0, rot_ref.shape[0] // HD, head, 0)
    dq_ref[...] = out_ref[...].T.astype(BF)


def attend(q_down, k_all, v_all, tables):
    cosine, sines, keys_at, places, length = tables
    width, rows = q_down.shape
    return pl.pallas_call(
        attend_kernel,
        out_shape=(
            jax.ShapeDtypeStruct((rows, width), BF),
            jax.ShapeDtypeStruct((width, rows), BF),
            jax.ShapeDtypeStruct((width // HD, rows), F32),
        ),
        in_specs=[VMEM] * 8,
        out_specs=(VMEM,) * 3,
        scratch_shapes=[pltpu.VMEM((k_all.shape[0], rows), F32), pltpu.VMEM((width, rows), F32)],
        compiler_params=pltpu.CompilerParams(vmem_limit_bytes=VMEM_LIMIT),
        cost_estimate=pl.CostEstimate(
            flops=16 * width * rows * k_all.shape[0], bytes_accessed=60_000_000, transcendentals=0
        ),
        name="attend",
    )(q_down, k_all, v_all.T, cosine, sines, keys_at[:, None], places[None], length)


def attend_back(rotated, k_all, v_all, d_down, lse, tables):
    cosine, sines, keys_at, places, length = tables
    width, rows = rotated.shape
    return pl.pallas_call(
        attend_back_kernel,
        out_shape=(
            jax.ShapeDtypeStruct((rows, width), BF),
            jax.ShapeDtypeStruct(k_all.shape, F32),
            jax.ShapeDtypeStruct(k_all.shape, F32),
        ),
        in_specs=[VMEM] * 11,
        out_specs=(VMEM,) * 3,
        scratch_shapes=[pltpu.VMEM((k_all.shape[0], rows), F32), pltpu.VMEM((width, rows), F32)],
        compiler_params=pltpu.CompilerParams(vmem_limit_bytes=VMEM_LIMIT),
        cost_estimate=pl.CostEstimate(
            flops=40 * width * rows * k_all.shape[0], bytes_accessed=80_000_000, transcendentals=0
        ),
        name="attend_back",
    )(
        rotated, k_all, k_all.T, v_all, d_down, lse, cosine, sines,
        keys_at[:, None], places[None], length,
    )


def load_blocks(w_refs, w_layer, low, high, target_of, sem):
    shard, home = lax.axis_index("gx"), lax.axis_index("section") == w_layer
    waits = []
    for j in range(4):

        def copy(ref):
            source = ref.at[: ref.shape[0] - GAIN_ROWS, low:high]
            return pltpu.make_async_copy(source, target_of(j), sem.at[j])

        waits.append(copy(w_refs[0].at[j]))
        if len(w_refs) == 1:
            waits[j].start()
        else:
            pl.when(shard != j)(waits[j].start)
            pl.when((shard == j) & home)(copy(w_refs[1]).start)
            pl.when((shard == j) & jnp.logical_not(home))(copy(w_refs[2]).start)
    return waits


def meet_near(*others):
    near = {"gx": lax.axis_index("gx") ^ 1}
    barrier = pltpu.get_barrier_semaphore()
    for peer in (near, *others):
        pl.semaphore_signal(barrier, inc=1, device_id=peer, device_id_type=MESH)
    pl.semaphore_wait(barrier, 1 + len(others))
    return near


def attend_whole_kernel(
    w_layer, listed,
    h_ref, gain_ref, cos_ref, sin_ref, key_ref, query_ref, length_ref, *rest,
):
    w_refs, rest = rest[:listed], rest[listed:]
    (
        heads_ref, normed_ref, ms_ref, rot_ref, lse_ref, k_ref, kt_ref, v_ref,
        w_all, bias_ref, out_ref, q_ref, vt_ref, kv_mine, kv_far, w_sem, send_sem, recv_sem,
    ) = rest
    rows, width = h_ref.shape
    block = width // 4
    q_width = q_ref.shape[0]
    waits = load_blocks(
        w_refs, w_layer, 0, q_width + 2 * HD, lambda j: w_all.at[j * block : (j + 1) * block], w_sem
    )
    near = meet_near()

    def norm(i, carry):
        here = pl.ds(pl.multiple_of(i * 128, 128), 128)
        values = h_ref[here, :].astype(F32)
        square = jnp.mean(values * values, axis=1, keepdims=True)
        ms_ref[here, :] = square
        normed_ref[here, :] = (values * lax.rsqrt(square + EPS) * gain_ref[...]).astype(BF)
        return carry

    lax.fori_loop(0, rows // 128, norm, 0)
    for wait in waits:
        wait.wait()
    kv = dot_to(normed_ref[...], w_all[:, q_width:], ((1,), (0,))).T
    kv = jnp.concatenate([rope_down(kv[:HD], cos_ref[...], sin_ref[...]), kv[HD:]], axis=0)
    kv_mine[...] = kv.T.astype(BF)
    copy = pltpu.make_async_remote_copy(
        src_ref=kv_mine, dst_ref=kv_far, send_sem=send_sem, recv_sem=recv_sem,
        device_id=near, device_id_type=MESH,
    )
    copy.start()
    q_ref[...] = dot_to(normed_ref[...], w_all[:, :q_width], ((1,), (0,))).T
    fill_bias(bias_ref, key_ref, query_ref, length_ref)
    copy.wait()
    for n, ref in enumerate((kv_mine, kv_far)):
        here = pl.ds(n * rows, rows)
        k_ref[here, :] = ref[:, :HD]
        v_ref[here, :] = ref[:, HD:]
        down = ref[...].astype(F32).T.astype(BF)
        kt_ref[:, here] = down[:HD]
        vt_ref[:, here] = down[HD:]

    def head(h, carry):
        here = pl.ds(pl.multiple_of(h * HD, HD), HD)
        rotated = rope_down(q_ref[here, :], cos_ref[...], sin_ref[...]).astype(BF)
        rot_ref[here, :] = rotated
        scaled = (rotated.astype(F32) * HD ** (-0.5)).astype(BF)
        scores = dot_to(k_ref[...], scaled, ((1,), (0,))) + bias_ref[...]
        top = jnp.max(scores, axis=0, keepdims=True)
        exponent = jnp.exp(scores - top)
        total = jnp.sum(exponent, axis=0, keepdims=True)
        probs = (exponent * (1.0 / total)).astype(BF)
        out_ref[here, :] = dot_to(vt_ref[...], probs, ((1,), (0,)))
        lse_ref[pl.ds(h, 1), :] = top + jnp.log(total)
        return carry

    lax.fori_loop(0, q_width // HD, head, 0)
    heads_ref[...] = out_ref[...].T.astype(BF)


def attend_whole_back_kernel(
    w_layer, listed, crosses,
    e1_ref, rot_ref, lse_ref, k_ref, kt_ref, v_ref, cos_ref, sin_ref, key_ref, query_ref,
    length_ref, *rest,
):
    w_refs, rest = rest[:listed], rest[listed:]
    if crosses:
        source_ref, d_qkv_ref, crossed_ref, *rest, x_send, x_recv = rest
    else:
        d_qkv_ref, *rest = rest
    (
        w_all, bias_ref, d_ref, out_ref, dk_ref, dv_ref, dkv_send, dkv_far,
        w_sem, send_sem, recv_sem,
    ) = rest
    rows, width = e1_ref.shape
    block = width // 4
    q_width = rot_ref.shape[0]
    low = q_width + 2 * HD
    waits = load_blocks(w_refs, w_layer, low, low + block, lambda j: w_all.at[j], w_sem)
    section = lax.axis_index("section")
    x_peer = {"section": 1 - section}
    near = meet_near(x_peer) if crosses else meet_near()

    def x_copy():
        return pltpu.make_async_remote_copy(
            src_ref=source_ref, dst_ref=crossed_ref, send_sem=x_send, recv_sem=x_recv,
            device_id=x_peer, device_id_type=MESH,
        )

    if crosses:
        pl.when(section != w_layer)(lambda: x_copy().start())
    fill_bias(bias_ref, key_ref, query_ref, length_ref)
    dk_ref[...] = jnp.zeros_like(dk_ref)
    dv_ref[...] = jnp.zeros_like(dv_ref)
    scaling = HD ** (-0.5)
    for wait in waits:
        wait.wait()
    d_ref[...] = sum(
        dot_to(w_all[j], e1_ref[:, j * block : (j + 1) * block], ((1,), (1,))) for j in range(4)
    ).astype(BF)

    def head(h, carry):
        here = pl.ds(pl.multiple_of(h * HD, HD), HD)
        scaled = (rot_ref[here, :].astype(F32) * scaling).astype(BF)
        scores = dot_to(k_ref[...], scaled, ((1,), (0,))) + bias_ref[...]
        probs = jnp.exp(scores - lse_ref[pl.ds(h, 1), :])
        d_probs = dot_to(v_ref[...], d_ref[here, :], ((1,), (0,)))
        delta = jnp.sum(probs * d_probs, axis=0, keepdims=True)
        d_scores = (probs * (d_probs - delta)).astype(BF)
        dk_ref[...] += dot_to(d_scores, scaled, ((1,), (1,)))
        dv_ref[...] += dot_to(probs.astype(BF), d_ref[here, :], ((1,), (1,)))
        dq = dot_to(kt_ref[...], d_scores, ((1,), (0,))) * scaling
        out_ref[here, :] = rope_down(dq, cos_ref[...], -sin_ref[...])
        return carry

    lax.fori_loop(0, q_width // HD, head, 0)
    dkv_send[:, :HD] = dk_ref[rows:, :]
    dkv_send[:, HD:] = dv_ref[rows:, :]
    copy = pltpu.make_async_remote_copy(
        src_ref=dkv_send, dst_ref=dkv_far, send_sem=send_sem, recv_sem=recv_sem,
        device_id=near, device_id_type=MESH,
    )
    copy.start()
    d_qkv_ref[:, :q_width] = out_ref[...].T.astype(BF)
    copy.wait()
    down = (dkv_far[...].T)
    dk = rope_down(dk_ref[:rows, :].T + down[:HD], cos_ref[...], -sin_ref[...])
    dkv = jnp.concatenate([dk, dv_ref[:rows, :].T + down[HD:]], axis=0)
    d_qkv_ref[:, q_width:] = dkv.T.astype(BF)
    if crosses:
        pl.when(section != w_layer)(lambda: x_copy().wait_send())
        pl.when(section == w_layer)(lambda: x_copy().wait_recv())


def attend_whole(h, gain, w_attn, low, tables, w_layer, ident):
    cosine, sines, keys_at, places, length = tables
    rows, width = h.shape
    keys, q_width = keys_at.shape[0], low - 2 * HD
    w_list = list(w_attn) if isinstance(w_attn, tuple) else [w_attn]
    outs = [
        ((rows, q_width), BF), ((rows, width), BF), ((rows, 1), F32), ((q_width, rows), BF),
        ((q_width // HD, rows), F32), ((keys, HD), BF), ((HD, keys), BF), ((keys, HD), BF),
    ]
    return pl.pallas_call(
        functools.partial(attend_whole_kernel, w_layer, len(w_list)),
        out_shape=tuple(jax.ShapeDtypeStruct(*o) for o in outs),
        in_specs=[VMEM] * 7 + [ANY] * len(w_list),
        out_specs=(VMEM,) * 8,
        scratch_shapes=[
            pltpu.VMEM((width, low), BF),
            pltpu.VMEM((keys, rows), F32),
            pltpu.VMEM((q_width, rows), F32),
            pltpu.VMEM((q_width, rows), F32),
            pltpu.VMEM((HD, keys), BF),
            pltpu.VMEM((rows, 2 * HD), BF),
            pltpu.VMEM((rows, 2 * HD), BF),
            pltpu.SemaphoreType.DMA((4,)),
            pltpu.SemaphoreType.DMA,
            pltpu.SemaphoreType.DMA,
        ],
        compiler_params=pltpu.CompilerParams(
            collective_id=ident, has_side_effects=True, vmem_limit_bytes=VMEM_LIMIT
        ),
        cost_estimate=pl.CostEstimate(
            flops=16 * q_width * rows * keys, bytes_accessed=70_000_000, transcendentals=0
        ),
        name="attend_whole",
    )(h, gain, cosine, sines, keys_at[:, None], places[None], length, *w_list)


def attend_whole_back(
    e1, rotated, lse, k_all, kt_all, v_all, w_attn, tables, w_layer, ident, cross
):
    cosine, sines, keys_at, places, length = tables
    q_width, rows = rotated.shape
    keys, width = keys_at.shape[0], e1.shape[1]
    w_list = list(w_attn) if isinstance(w_attn, tuple) else [w_attn]
    crossing_specs = [jax.ShapeDtypeStruct(x.shape, BF) for x in cross]
    return pl.pallas_call(
        functools.partial(attend_whole_back_kernel, w_layer, len(w_list), len(cross)),
        out_shape=(jax.ShapeDtypeStruct((rows, q_width + 2 * HD), BF), *crossing_specs),
        in_specs=[VMEM] * 11 + [ANY] * (len(w_list) + len(cross)),
        out_specs=(VMEM, *[ANY] * len(cross)),
        scratch_shapes=[
            pltpu.VMEM((4, q_width, width // 4), BF),
            pltpu.VMEM((keys, rows), F32),
            pltpu.VMEM((q_width, rows), BF),
            pltpu.VMEM((q_width, rows), F32),
            pltpu.VMEM((keys, HD), F32),
            pltpu.VMEM((keys, HD), F32),
            pltpu.VMEM((rows, 2 * HD), F32),
            pltpu.VMEM((rows, 2 * HD), F32),
            pltpu.SemaphoreType.DMA((4,)),
            pltpu.SemaphoreType.DMA,
            pltpu.SemaphoreType.DMA,
        ]
        + [pltpu.SemaphoreType.DMA] * 2 * len(cross),
        compiler_params=pltpu.CompilerParams(
            collective_id=ident, has_side_effects=True, vmem_limit_bytes=VMEM_LIMIT
        ),
        cost_estimate=pl.CostEstimate(
            flops=40 * q_width * rows * keys, bytes_accessed=90_000_000, transcendentals=0
        ),
        name="attend_whole_back",
    )(
        e1, rotated, lse, k_all, kt_all, v_all, cosine, sines, keys_at[:, None], places[None],
        length, *w_list, *cross,
    )


def line_kernel(
    kind, masked, low, high, deps, gathers, layer, exchange, triples, w_layer, crosses, homing,
    gain_ref, resid_ref, valid_ref, h_ref, square_ref, *rest,
):
    forward = kind in ("out", "mlp")
    wide = kind in ("mlp", "mlp_back")
    if kind == "mlp":
        lhs_refs = []
    elif kind == "mlp_back":
        lhs_refs, rest = rest[:4], rest[4:]
    else:
        lhs_refs, rest = rest[:1], rest[1:]
    w_count = 3 if wide else 1
    w_refs = []
    for triple in triples:
        w_refs.append(rest[: 3 if triple else 1])
        rest = rest[3 if triple else 1 :]
    rest = rest[deps:]
    base_refs, rest = rest[: 2 * gathers], rest[2 * gathers :]
    cross_refs, rest = rest[: len(crosses)], rest[len(crosses) :]
    out_ref, rest = rest[0], rest[1:]
    if kind == "mlp":
        normed_ref, ms_ref, gate_ref, up_ref, hidden_ref = rest[:5]
        rest = rest[5:]
    elif kind == "mlp_back":
        product_refs, rest = rest[:3], rest[3:]
        arrived_refs, rest = rest[:exchange], rest[exchange:]
    block_refs, rest = rest[:gathers], rest[gathers:]
    crossed_refs, rest = rest[: len(crosses)], rest[len(crosses) :]
    if homing:
        home_ref, home_send, home_recv = rest[0], *rest[-2:]
        rest = rest[1:-2]
    if crosses:
        x_send, x_recv = rest[-2:]
        rest = rest[:-2]
    w_alls, rest = rest[:w_count], rest[w_count:]
    (
        part, from_end, from_mid, pair,
        w_sem, up_send, up_recv, mid_send, mid_recv, fin_send, fin_recv,
    ) = rest[:11]
    if gathers:
        far_send, far_recv, near_send, near_recv, cross_send, cross_recv = rest[11:]
    if kind == "mlp_back":
        (
            d_gate_ref, d_up_ref, far_normed, far_dm, far_hidden, far_d_gate, far_d_up, stage,
            give_sem, take_sem, stage_sem,
        ) = rest[11:22]
    if exchange:
        y_stage, y_send, y_recv = rest[22:]
    shard = lax.axis_index("gx")
    far, near = shard ^ 2, shard ^ 1
    section = lax.axis_index("section")
    rows, width = resid_ref.shape
    columns = width // 4
    count = rows // CHUNK
    z = lax.axis_index("gy")
    middle = (z == 1) | (z == 2)
    end_of = jnp.where(z == 1, 0, 3)
    mid_of = jnp.where(z == 0, 1, 2)
    across = 3 - z

    def loading(w, j, cut_of, target, slot):
        whole = w_refs[w]
        copies = [(None, pltpu.make_async_copy(cut_of(whole[0].at[j]), target, w_sem.at[slot]))]
        if triples[w]:
            home = section == w_layer
            copies = [(shard != j, copies[0][1])]
            for ref, holds in zip(whole[1:], (home, jnp.logical_not(home))):
                copy = pltpu.make_async_copy(cut_of(ref), target, w_sem.at[slot])
                copies.append(((shard == j) & holds, copy))
        return copies

    loads, downs = [], []
    if wide:
        hidden_width = w_alls[0].shape[1]
        for x0 in range(0, hidden_width, 512):
            x1 = min(x0 + 512, hidden_width)
            for w in range(2):
                for j in range(4):
                    target = w_alls[w].at[j * columns : (j + 1) * columns, x0:x1]
                    loads.append(loading(w, j, lambda ref: ref.at[:, x0:x1], target, len(loads)))
        for j in range(4):
            downs.append(loading(2, j, lambda ref: ref, w_alls[2].at[j], len(loads) + j))
    else:
        for j in range(4):
            cut_of = lambda ref: ref.at[: ref.shape[0] - GAIN_ROWS, low:high]
            loads.append(loading(0, j, cut_of, w_alls[0].at[j], j))
    for load in downs + loads if kind == "mlp_back" else loads + downs:
        for holds, copy in load:
            if holds is None:
                copy.start()
            else:
                pl.when(holds)(copy.start)
    loads, downs = [x[0][1] for x in loads], [x[0][1] for x in downs]

    barrier = pltpu.get_barrier_semaphore()
    peers = []
    if gathers:
        peers = [{"gx": far}, {"gx": near}, {"section": 1 - section}]
    elif kind == "mlp_back":
        peers = [{"gx": near}] + [{"gx": far}] * (exchange > 0)
    if crosses:
        assert not gathers
        peers.append({"section": 1 - section})
    beside = len(peers)
    for peer in peers:
        pl.semaphore_signal(barrier, inc=1, device_id=peer, device_id_type=MESH)

    @pl.when(middle)
    def _():
        pl.semaphore_signal(barrier, inc=1, device_id={"gy": end_of}, device_id_type=MESH)
        pl.semaphore_signal(barrier, inc=1, device_id={"gy": across}, device_id_type=MESH)
        pl.semaphore_wait(barrier, 2 + beside)

    @pl.when(jnp.logical_not(middle))
    def _():
        pl.semaphore_signal(barrier, inc=1, device_id={"gy": mid_of}, device_id_type=MESH)
        pl.semaphore_wait(barrier, 1 + beside)

    x_peer = {"section": 1 - section}

    def x_copy(k):
        return pltpu.make_async_remote_copy(
            src_ref=cross_refs[k], dst_ref=crossed_refs[k], send_sem=x_send.at[k],
            recv_sem=x_recv.at[k], device_id=x_peer, device_id_type=MESH,
        )

    def home_copy(rows_here):
        return pltpu.make_async_remote_copy(
            src_ref=out_ref.at[rows_here, pl.ds(pl.multiple_of(z * columns, columns), columns)],
            dst_ref=home_ref.at[rows_here, :], send_sem=home_send, recv_sem=home_recv,
            device_id=x_peer, device_id_type=MESH,
        )

    def home_start(i):
        if homing:
            here = pl.ds(pl.multiple_of(i * CHUNK, CHUNK), CHUNK)
            pl.when(section != w_layer)(lambda: home_copy(here).start())

    def x_sends(k):
        return section != crosses[k] if crosses[k] < 2 else section >= 0

    def x_takes(k):
        return section == crosses[k] if crosses[k] < 2 else section >= 0

    for k in range(len(crosses)):
        pl.when(x_sends(k))(lambda k=k: x_copy(k).start())

    def half_of(ref, k, which):
        size = base_refs[2 * k].shape[0] // 2
        return ref.at[pl.ds(pl.multiple_of(which * size, 16), size), :]

    def far_copy(k, source):
        return pltpu.make_async_remote_copy(
            src_ref=half_of(source, k, section),
            dst_ref=half_of(block_refs[k].at[shard], k, section),
            send_sem=far_send.at[k], recv_sem=far_recv.at[k],
            device_id={"gx": far}, device_id_type=MESH,
        )

    def near_copy(k, source):
        return pltpu.make_async_remote_copy(
            src_ref=source, dst_ref=block_refs[k].at[shard], send_sem=near_send.at[3 * k],
            recv_sem=near_recv.at[3 * k], device_id={"gx": near}, device_id_type=MESH,
        )

    def cross_copy(k):
        rows_here = half_of(block_refs[k].at[far], k, section)
        return pltpu.make_async_remote_copy(
            src_ref=rows_here, dst_ref=rows_here, send_sem=cross_send.at[k],
            recv_sem=cross_recv.at[k], device_id=x_peer, device_id_type=MESH,
        )

    def pass_copy(k, late):
        rows_here = half_of(block_refs[k].at[far], k, 1 - section if late else section)
        return pltpu.make_async_remote_copy(
            src_ref=rows_here, dst_ref=rows_here, send_sem=near_send.at[3 * k + 1 + late],
            recv_sem=near_recv.at[3 * k + 1 + late], device_id={"gx": near}, device_id_type=MESH,
        )

    at_home = section == layer

    def from_base(k, starts):
        for ref, holds in zip(base_refs[2 * k : 2 * k + 2], (at_home, jnp.logical_not(at_home))):

            @pl.when(holds)
            def _():
                for make in starts:
                    make(k, ref).start()

    def gather_middle(k):
        far_copy(k, base_refs[2 * k]).wait_recv()
        cross_copy(k).start()
        pass_copy(k, 0).start()

    def gather_late(k):
        cross_copy(k).wait_recv()
        pass_copy(k, 1).start()

    if gathers:
        from_base(0, [far_copy])
    for k in range(gathers):
        from_base(k, [near_copy])

    half = rows // STEPS
    core = lax.rem(shard, 2)

    def give(slot, source, target):
        return pltpu.make_async_remote_copy(
            src_ref=source, dst_ref=target, send_sem=give_sem.at[slot],
            recv_sem=take_sem.at[slot], device_id={"gx": near}, device_id_type=MESH,
        )

    def chip_columns(ref, y, of):
        return ref.at[:, pl.ds(pl.multiple_of((2 * y + of) * columns, columns), columns)]

    def step_rows(ref, step):
        return ref.at[pl.ds(pl.multiple_of(step * half, half), half), :]

    if kind == "mlp_back":
        saved_gate, saved_up, saved_normed, saved_hidden = lhs_refs
        early = [give(0, saved_hidden, far_hidden)]
        for y in range(2):
            early.append(give(1 + y, chip_columns(resid_ref, y, 1 - core), far_dm.at[y]))
        for y in range(2):
            early.append(give(3 + y, chip_columns(saved_normed, y, 1 - core), far_normed.at[y]))
        for copy in early:
            copy.start()

    def give_step(step):
        return [
            give(5 + step, step_rows(d_gate_ref, step), step_rows(far_d_gate, step)),
            give(5 + STEPS + step, step_rows(d_up_ref, step), step_rows(far_d_up, step)),
        ]

    if not wide:
        for load in loads:
            load.wait()

    def at_first(step, copies):
        @pl.when(step == 0)
        def _():
            for copy in copies:
                copy.wait()

    def rows_at(ref, i):
        return ref.at[pl.ds(pl.multiple_of(i * CHUNK, CHUNK), CHUNK), :]

    def up_copy(i):
        return pltpu.make_async_remote_copy(
            src_ref=rows_at(part, i), dst_ref=rows_at(from_end, i), send_sem=up_send.at[i],
            recv_sem=up_recv.at[i], device_id={"gy": mid_of}, device_id_type=MESH,
        )

    def mid_copy(i):
        return pltpu.make_async_remote_copy(
            src_ref=rows_at(pair, i), dst_ref=rows_at(from_mid, i), send_sem=mid_send.at[i],
            recv_sem=mid_recv.at[i], device_id={"gy": across}, device_id_type=MESH,
        )

    def fin_copy(i):
        return pltpu.make_async_remote_copy(
            src_ref=rows_at(out_ref, i), dst_ref=rows_at(out_ref, i), send_sem=fin_send.at[i],
            recv_sem=fin_recv.at[i], device_id={"gy": end_of}, device_id_type=MESH,
        )

    def dot(left, right, transposed=False):
        dims = (((1,), (1 if transposed else 0,)), ((), ()))
        return lax.dot_general(left, right, dims, preferred_element_type=F32)

    def spans(extent):
        return [(x, min(x + 512, extent)) for x in range(0, extent, 512)]

    if wide:
        w_gate, w_up, w_down = w_alls

    def product(step, carry):
        here = pl.ds(pl.multiple_of(step * half, half), half)
        if kind == "mlp":
            values = resid_ref[here, :].astype(F32)
            square = jnp.mean(values * values, axis=1, keepdims=True)
            ms_ref[here, :] = square
            normed_ref[here, :] = (values * lax.rsqrt(square + EPS) * gain_ref[...]).astype(BF)
            for n, (x0, x1) in enumerate(spans(w_gate.shape[1])):
                at_first(step, loads[8 * n : 8 * n + 8])
                gate = dot(normed_ref[here, :], w_gate[:, x0:x1])
                up = dot(normed_ref[here, :], w_up[:, x0:x1])
                gate_ref[here, x0:x1] = gate.astype(BF)
                up_ref[here, x0:x1] = up.astype(BF)
                hidden_ref[here, x0:x1] = (gate * jax.nn.sigmoid(gate) * up).astype(BF)
        if kind == "mlp_back":
            at_first(step, downs)
            for x0, x1 in spans(w_gate.shape[1]):
                d_hidden = sum(
                    dot(resid_ref[here, j * columns : (j + 1) * columns], w_down[j, x0:x1, :], True)
                    for j in range(4)
                )
                gate = saved_gate[here, x0:x1].astype(F32)
                up = saved_up[here, x0:x1].astype(F32)
                sigmoid = jax.nn.sigmoid(gate)
                d_up_ref[here, x0:x1] = (d_hidden * (gate * sigmoid)).astype(BF)
                d_gate_ref[here, x0:x1] = (
                    d_hidden * up * sigmoid * (1.0 + gate * (1.0 - sigmoid))
                ).astype(BF)
            for copy in give_step(step):
                copy.start()
        if wide:
            at_first(step, downs if kind == "mlp" else loads)
        for j in range(4):
            span = slice(j * columns, (j + 1) * columns)
            if kind == "out":
                value = dot(lhs_refs[0][here, :], w_alls[0][j])
            elif kind == "mlp":
                value = dot(hidden_ref[here, :], w_down[j])
            elif kind == "mlp_back":
                value = dot(d_gate_ref[here, :], w_gate[span, :], True)
                value += dot(d_up_ref[here, :], w_up[span, :], True)
            else:
                value = dot(lhs_refs[0][here, :], w_alls[0][j], True)
            part[here, span] = value.astype(BF)

        @pl.when(jnp.logical_not(middle))
        def _():
            def send(i, inner):
                up_copy(step * (count // STEPS) + i).start()
                return inner

            lax.fori_loop(0, count // STEPS, send, 0)

        return carry

    lax.fori_loop(0, STEPS, product, 0)

    def finish(i):
        mid_copy(i).wait_recv()
        here = pl.ds(pl.multiple_of(i * CHUNK, CHUNK), CHUNK)
        total = pair[here, :].astype(F32) + from_mid[here, :].astype(F32)
        resid = resid_ref[here, :].astype(F32)
        if forward:
            result = resid + total
            if masked:
                result = result * valid_ref[here, :]
        else:
            values = h_ref[here, :].astype(F32)
            scaled = total * gain_ref[...]
            ratio = lax.rsqrt(square_ref[here, :] + EPS)
            mean_term = jnp.sum(scaled * values, axis=1, keepdims=True) * (1.0 / width)
            result = resid + ratio * scaled - values * (ratio * ratio * ratio) * mean_term
        out_ref[here, :] = result.astype(BF)
        fin_copy(i).start()
        home_start(i)

    tile = columns // 2

    def tile_rows(sub):
        return pl.ds(pl.multiple_of(sub % 2 * tile, tile), tile)

    def stage_copy(number, sub, slot):
        target = product_refs[number].at[sub // 2, tile_rows(sub), :]
        return pltpu.make_async_copy(stage.at[slot], target, stage_sem.at[slot])

    def y_copy(number, sub, slot):
        return pltpu.make_async_remote_copy(
            src_ref=y_stage.at[2 * number + slot], dst_ref=arrived_refs[number].at[tile_rows(sub), :],
            send_sem=y_send.at[2 * number + slot], recv_sem=y_recv.at[2 * number + slot],
            device_id={"gx": far}, device_id_type=MESH,
        )

    def gradient_tile(number, sub):
        slot = sub % 2
        left, far_left, right, far_right = (
            (resid_ref, far_dm, saved_hidden, far_hidden),
            (saved_normed, far_normed, d_gate_ref, far_d_gate),
            (saved_normed, far_normed, d_up_ref, far_d_up),
        )[number]

        @pl.when(sub == 0)
        def _():
            waits = [early[:3], early[3:] + give_all[:STEPS], give_all[STEPS:]][number]
            for copy in waits:
                copy.wait_recv()

        if number >= exchange:

            @pl.when((sub >= 2) | (number > 0))
            def _():
                stage_copy(number, sub, slot).wait()

        elif number > 0:

            @pl.when(sub >= 2)
            def _():
                stage_copy(number, sub - 2, slot).wait()

        y = sub // 2
        if number < exchange:
            y = jnp.where(sub < 2, 1 - lax.div(shard, 2), lax.div(shard, 2))
        start = (y * 2 + core) * columns + sub % 2 * tile
        mine = left[:, pl.ds(pl.multiple_of(start, tile), tile)]
        theirs = far_left[y, :, tile_rows(sub)]
        value = dot_to(mine, right[...], ((0,), (0,))) + dot_to(theirs, far_right[...], ((0,), (0,)))
        if number < exchange:

            @pl.when(sub < 2)
            def _():
                y_stage[2 * number + slot] = value.astype(BF)
                y_copy(number, sub, slot).start()

            @pl.when(sub >= 2)
            def _():
                stage[slot] = value.astype(BF)
                stage_copy(number, sub - 2, slot).start()

        else:
            stage[slot] = value.astype(BF)
            stage_copy(number, sub, slot).start()

    if kind == "mlp_back":
        give_all = [x for pair in zip(*(give_step(n) for n in range(STEPS))) for x in pair]

    def beside_step(i, ahead=0):
        pass_on(i + ahead)
        if kind == "mlp_back":
            for number in range(3):
                first = 3 + 4 * number

                @pl.when((i >= first) & (i < first + 4))
                def _():
                    gradient_tile(number, i - first)

    def pass_on(i):
        if gathers == 2:
            at(2, i, lambda: from_base(1, [far_copy]))
            at(6, i, lambda: gather_middle(0))
            at(10, i, lambda: gather_middle(1))
            at(11, i, lambda: gather_late(0))
            at(15, i, lambda: gather_late(1))

    def at(sixteenth, i, action):
        pl.when(i == count * sixteenth // 16)(action)

    @pl.when(middle)
    def _():
        def step(i, carry):
            up_copy(i).wait_recv()
            here = pl.ds(pl.multiple_of(i * CHUNK, CHUNK), CHUNK)
            pair[here, :] = (part[here, :].astype(F32) + from_end[here, :].astype(F32)).astype(BF)
            mid_copy(i).start()

            @pl.when(i >= 1)
            def _():
                finish(i - 1)

            beside_step(i)
            return carry

        lax.fori_loop(0, count, step, 0)
        finish(count - 1)

        def drain(i, carry):
            mid_copy(i).wait_send()
            fin_copy(i).wait_send()
            return carry

        lax.fori_loop(0, count, drain, 0)

    @pl.when(jnp.logical_not(middle))
    def _():
        if gathers == 2:
            from_base(1, [far_copy])

        def drain(i, carry):
            up_copy(i).wait_send()
            fin_copy(i).wait_recv()
            home_start(i)
            beside_step(i, 3)
            return carry

        lax.fori_loop(0, count, drain, 0)

    if kind == "mlp_back":
        for slot in range(2):
            stage_copy(2, 2 + slot, slot).wait()
        for copy in early + give_all:
            copy.wait_send()
        for number in range(exchange):
            for slot in range(2):
                y_copy(number, slot, slot).wait()
    if homing:
        every = pl.ds(0, rows)
        pl.when(section != w_layer)(lambda: home_copy(every).wait_send())
        pl.when(section == w_layer)(lambda: home_copy(every).wait_recv())
    for k in range(len(crosses)):
        pl.when(x_sends(k))(lambda k=k: x_copy(k).wait_send())
        pl.when(x_takes(k))(lambda k=k: x_copy(k).wait_recv())
    for k in range(gathers):
        far_copy(k, base_refs[2 * k]).wait_send()
        near_copy(k, base_refs[2 * k]).wait()
        cross_copy(k).wait_send()
        pass_copy(k, 0).wait()
        pass_copy(k, 1).wait()


def line_sum(kind, ident, resid, weights, lhs=(), gain=None, valid=None, back=None, low=0, high=0, deps=(), bases=(), layer=0, exchange=0, w_layer=0, crosses=(), homing=False):
    rows, width = resid.shape
    one = jnp.ones((rows, 1), F32)
    h, square = back if back is not None else (jnp.zeros((16, 128), BF), jnp.zeros((8, 1), F32))
    gain = jnp.zeros((1, width), F32) if gain is None else gain
    wide = kind in ("mlp", "mlp_back")
    hidden = 0
    if wide:
        hidden = (weights[2][0] if isinstance(weights[2], tuple) else weights[2]).shape[1]
    w_scratch = []
    triples = [isinstance(w, tuple) for w in weights]
    w_flat = [x for w in weights for x in (w if isinstance(w, tuple) else (w,))]
    for i, w in enumerate(weights):
        _, depth, across = (w[0] if isinstance(w, tuple) else w).shape
        if wide and i < 2:
            w_scratch.append(pltpu.VMEM((width, across), BF))
        else:
            shape = (4, depth, across) if wide else (4, depth - GAIN_ROWS, high - low)
            w_scratch.append(pltpu.VMEM(shape, BF))
    outs, products, beside = [((rows, width), BF)], [], []
    if kind == "mlp":
        outs += [((rows, width), BF), ((rows, 1), F32)] + [((rows, hidden), BF)] * 3
    elif kind == "mlp_back":
        products = [((1 if n < exchange else 2, width // 4, hidden), BF) for n in range(3)]
        products += [((width // 4, hidden), BF)] * exchange
        half_block = pltpu.VMEM((2, rows, width // 4), BF)
        beside = [pltpu.VMEM((rows, hidden), BF)] * 2 + [half_block] * 2
        beside += [pltpu.VMEM((rows, hidden), BF)] * 3 + [pltpu.VMEM((2, width // 8, hidden), BF)]
        beside += [pltpu.SemaphoreType.DMA((n,)) for n in (5 + 2 * STEPS, 5 + 2 * STEPS, 2)]
        if exchange:
            beside += [pltpu.VMEM((2 * exchange, width // 8, hidden), BF)]
            beside += [pltpu.SemaphoreType.DMA((2 * exchange,))] * 2
    blocks = [((4,) + base[0].shape, BF) for base in bases]
    pairs = [x for base in bases for x in base]
    crossed = [(x[0].shape, BF) for x in crosses] + [((rows, width // 4), BF)] * homing
    depth = 3 * hidden if wide else lhs[0].shape[1]
    count = rows // CHUNK
    dma = pltpu.SemaphoreType.DMA
    return pl.pallas_call(
        functools.partial(
            line_kernel, kind, valid is not None, low, high, len(deps), len(bases), layer, exchange,
            triples, w_layer, [x[1] for x in crosses], homing,
        ),
        out_shape=tuple(jax.ShapeDtypeStruct(*o) for o in outs + products + blocks + crossed),
        in_specs=[VMEM] * (5 + len(lhs)) + [ANY] * (len(w_flat) + len(deps) + len(pairs) + len(crosses)),
        out_specs=tuple([VMEM] * len(outs) + [ANY] * len(products + blocks + crossed)),
        scratch_shapes=w_scratch
        + [pltpu.VMEM((rows, width), BF)] * 4
        + [dma((8 * -(-hidden // 512) + 4,))]
        + [dma((count,))] * 6
        + [dma((n * len(bases),)) for n in (1, 1, 3, 3, 1, 1) if bases]
        + beside
        + [dma((len(crosses),))] * 2 * bool(crosses)
        + [dma] * 2 * homing,
        compiler_params=pltpu.CompilerParams(
            collective_id=ident, has_side_effects=True, vmem_limit_bytes=VMEM_LIMIT
        ),
        cost_estimate=pl.CostEstimate(
            flops=2 * rows * depth * width, bytes_accessed=200 * 1024 * 1024, transcendentals=0
        ),
        name="line_" + kind,
    )(
        gain, resid, one if valid is None else valid, h, square, *lhs, *w_flat, *deps, *pairs,
        *(x[0] for x in crosses),
    )


def plain_sum(total):
    return lax.psum(total.astype(BF), "gy").astype(F32)


def normed(h, gain):
    values = h.astype(F32)
    square = jnp.mean(values * values, axis=1, keepdims=True)
    return square, (values * lax.rsqrt(square + EPS) * gain).astype(BF)


def norm_back(d_normed, h, square, gain):
    values = h.astype(F32)
    ratio = lax.rsqrt(square + EPS)
    scaled = d_normed * gain
    mean_term = jnp.mean(scaled * values, axis=1, keepdims=True)
    return ratio * scaled - values * (ratio * ratio * ratio) * mean_term


def attention_forward(h, gain, w_attn, low, tables, ident, bases, layer, w_layer, deps=(), late=None):
    rows, width = h.shape
    high = low + width // lax.axis_size("gx")
    q_width = low - 2 * HD
    if fused():
        heads, n1, square, rotated, lse, k_all, kt_all, v_all = attend_whole(
            h, gain, w_attn, low, tables, w_layer, ident + 8
        )
        if late is not None:
            late = line_gather(late + heads[:1, :1] * 0)
            deps = (*deps, late)
        h1, *stacks = line_sum(
            "out", ident, h, [w_attn], (heads,), low=low, high=high,
            deps=deps, bases=bases, layer=layer, w_layer=w_layer,
        )
        blocks = [(x, *pair) for x, pair in zip(stacks, bases)]
    else:
        cosine, sines = tables[:2]
        square, n1 = normed(h, gain)
        q_down = mm(tall(cut(w_attn, 0, q_width)), n1, ((0,), (1,)))
        kv = mm(n1, tall(cut(w_attn, q_width, low)))
        k_rot = rope_down(kv[:, :HD].T, cosine, sines).T.astype(BF)
        kv = jnp.concatenate([k_rot, kv[:, HD:].astype(BF)], axis=1)
        kv_all = jnp.concatenate([kv, swap_pairs(kv, "gx")], axis=0)
        k_all, v_all = kv_all[:, :HD], kv_all[:, HD:]
        kt_all = k_all.T
        heads, rotated, lse = attend(q_down, k_all, v_all, tables)
        h1 = (h.astype(F32) + plain_sum(mm(heads, side(cut(w_attn, low, high))))).astype(BF)
        blocks = [gather_blocks(chosen(x, layer)) for x in bases]
        late = None if late is None else line_gather(late)
    if late is not None:
        blocks.append(late)
    return h1, square, blocks, (h, square, n1, rotated, lse, k_all, kt_all, v_all, heads)


def mlp_forward(h1, gain, weights, valid, ident, bases=(), layer=0, w_layer=0):
    if fused():
        result, n2, square, gate, up, hidden, *stacks = line_sum(
            "mlp", ident, h1, weights, gain=gain, valid=valid, bases=bases, layer=layer,
            w_layer=w_layer,
        )
        blocks = [(x, *pair) for x, pair in zip(stacks, bases)]
    else:
        square, n2 = normed(h1, gain)
        gate = mm(n2, tall(weights[0]))
        up = mm(n2, tall(weights[1]))
        hidden = (gate * jax.nn.sigmoid(gate) * up).astype(BF)
        gate, up = gate.astype(BF), up.astype(BF)
        result = h1.astype(F32) + plain_sum(mm(hidden, side(weights[2])))
        result = (result * valid).astype(BF)
        blocks = [gather_blocks(chosen(x, layer)) for x in bases]
    return result, square, blocks, (h1, square, n2, gate, up, hidden)


def mlp_backward(dm, gain, weights, saved, ident, w_layer, crosses=(), deps=(), exchange=1):
    h1, square, n2, gate, up, hidden = saved
    if fused():
        e1, *products = line_sum(
            "mlp_back", ident, dm, weights, (gate, up, n2, hidden), gain=gain,
            back=(h1, square), exchange=exchange, w_layer=w_layer, crosses=crosses, deps=deps,
        )
        return e1, products[:4], products[4:]
    gate, up = gate.astype(F32), up.astype(F32)
    d_hidden = mm(dm, side(weights[2]), ((1,), (1,)))
    sigmoid = jax.nn.sigmoid(gate)
    d_gate = (d_hidden * up * sigmoid * (1.0 + gate * (1.0 - sigmoid))).astype(BF)
    d_up = (d_hidden * (gate * sigmoid)).astype(BF)
    total = mm(d_gate, tall(weights[0]), ((1,), (1,))) + mm(d_up, tall(weights[1]), ((1,), (1,)))
    e1 = (dm.astype(F32) + norm_back(plain_sum(total), h1, square, gain)).astype(BF)
    turn = ((0,), (0,))
    products = [mm(dm, hidden, turn), mm(n2, d_gate, turn), mm(n2, d_up, turn)]
    return e1, [p.astype(BF) for p in products], crossing(crosses)


def crossing(crosses):
    pairs = ([(1, 0)], [(0, 1)], [(0, 1), (1, 0)])
    return [lax.ppermute(x, "section", pairs[way]) for x, way in crosses]


def mlp_sums(products):
    if not fused():
        return [shard_sum(p) for p in products]
    down, gate, up, arrived = products
    first = (down[0].astype(F32) + arrived.astype(F32)).astype(BF)
    return [first, chip_sum(gate), chip_sum(up)]


def attention_backward(e1, w_attn, low, tables, saved, w_layer, ident, cross=()):
    h, square, n1, rotated, lse, k_all, kt_all, v_all, heads = saved
    rows, width = h.shape
    if fused():
        d_qkv, *crossed = attend_whole_back(
            e1, rotated, lse, k_all, kt_all, v_all, w_attn, tables, w_layer, ident, cross
        )
    else:
        cosine, sines = tables[:2]
        w_o = side(cut(w_attn, low, low + width // lax.axis_size("gx")))
        d_down = mm(w_o, e1, ((1,), (1,))).astype(BF)
        dq, dk, dv = attend_back(rotated, k_all, v_all, d_down, lse, tables)
        dkv = jnp.concatenate([dk, dv], axis=1)
        dkv = dkv[:rows] + swap_pairs(dkv[rows:], "gx")
        dk = rope_down(dkv[:, :HD].T, cosine, -sines).T
        d_qkv = jnp.concatenate([dq, dk.astype(BF), dkv[:, HD:].astype(BF)], axis=1)
        crossed = crossing([(x, w_layer) for x in cross])
    turn = ((0,), (0,))
    products = [mm(n1, d_qkv, turn).astype(BF), mm(e1, heads, turn).astype(BF)]
    return d_qkv, jnp.concatenate(products, axis=1), crossed


def attention_end(d_qkv, e1, w_attn, gain, saved, ident, w_layer, deps, crosses):
    h, square = saved[:2]
    qkv_width = d_qkv.shape[1]
    if fused():
        grad, *crossed = line_sum(
            "back", ident, e1, [w_attn], (d_qkv,), gain=gain, back=(h, square),
            low=0, high=qkv_width, deps=deps, crosses=crosses, w_layer=w_layer, homing=True,
        )
        return grad, crossed[-1], crossed[:-1]
    total = plain_sum(mm(d_qkv, tall(cut(w_attn, 0, qkv_width)), ((1,), (1,))))
    grad = (e1.astype(F32) + norm_back(total, h, square, gain)).astype(BF)
    width = grad.shape[1] // lax.axis_size("gy")
    part = lax.dynamic_slice_in_dim(grad, lax.axis_index("gy") * width, width, 1)
    home, *crossed = crossing([(part, w_layer), *crosses])
    return grad, home, crossed


def on_device(
    hidden_in, out_grad, lengths, dealing, attn_gain, w_query, w_key, w_value, w_out,
    mlp_gain, w_gate, w_up, w_down,
):
    shards = lax.axis_size("gx")
    shard = lax.axis_index("gx")
    section = lax.axis_index("section")
    column = lax.axis_index("gy")
    core = shard % 2
    sequence = (shard // 2) * 2 + section
    span, width = hidden_in.shape
    half = span // 2
    seq_length = lax.dynamic_index_in_dim(lengths, sequence, keepdims=False)

    both = jnp.concatenate([hidden_in, out_grad], axis=1)
    mine = core_rows(both, core)
    theirs = swap_pairs(core_rows(both, 1 - core), "gx")
    mine = jnp.where(core == section, mine, theirs)
    h = line_gather(mine[:, :width])

    kv_head = column * (w_query.shape[2] // HD) // (QH // KVH)
    low = w_query.shape[2] + 2 * HD
    both_gains = jnp.stack([attn_gain[0], mlp_gain[0]])
    block_rows = both_gains.shape[1]
    attn_own = jnp.concatenate(
        [
            w_query[0],
            lax.dynamic_slice_in_dim(w_key[0], kv_head * HD, HD, 1),
            lax.dynamic_slice_in_dim(w_value[0], kv_head * HD, HD, 1),
            w_out[0],
        ],
        axis=1,
    )
    gain_rows = jnp.pad(both_gains, ((0, GAIN_ROWS - 2), (0, attn_own.shape[1] - block_rows)))
    attn_own = jnp.concatenate([attn_own, gain_rows + theirs[:1, :1] * 0], axis=0)
    own = (attn_own, w_gate[0], w_up[0], w_down[0])
    first = second = [(array, swap_pairs(array, "section")) for array in own]

    def gains_of(w_attn, pair):
        cut_of = lambda w: w[..., block_rows : block_rows + 2, :block_rows]
        rows = cut_of(w_attn[0] if isinstance(w_attn, tuple) else w_attn)
        if isinstance(w_attn, tuple):
            rows = with_own(rows, [cut_of(x) for x in pair], 1)
        return rows.transpose(1, 0, 2).reshape(2, 1, -1).astype(F32)

    here = core_rows(jnp.arange(span), core)
    there = core_rows(jnp.arange(span), 1 - core)
    keys_at = jnp.concatenate([here, there])
    valid = (here < seq_length)[:, None].astype(F32)
    tables = (*rope_tables(here), keys_at, here, seq_length.reshape(1, 1))

    attn0 = gather_blocks(chosen(first[0], 0) + h[:1, :1] * 0)
    gate0 = gather_blocks(chosen(first[1], 0) + h[:1, :1] * 0)
    gains0 = gains_of(attn0, first[0])
    h1, square_a, blocks, saved_a0 = attention_forward(
        h, gains0[0], attn0, low, tables, 0, first[2:], 0, 0, (gate0,), mine[:, width:]
    )
    d_out = blocks.pop()
    mlp0 = [gate0] + blocks
    h, square_m, (attn1, gate1), saved_m0 = mlp_forward(
        h1, gains0[1], mlp0, valid, 1, second[:2], 1
    )
    gains1 = gains_of(attn1, second[0])
    outputs, squares = [h], [square_a, square_m]
    h1, square_a, blocks, saved_a1 = attention_forward(
        h, gains1[0], attn1, low, tables, 2, second[2:], 1, 1
    )
    mlp1 = [gate1] + blocks
    h, square_m, _, saved_m1 = mlp_forward(h1, gains1[1], mlp1, valid, 3, w_layer=1)
    outputs.append(h)
    squares = jnp.concatenate(squares + [square_a, square_m], axis=1)
    rms = (jnp.sqrt(squares + EPS) * valid).T
    statistics = [rms[:2], rms[2:]]
    outputs = [lax.dynamic_slice_in_dim(x, column * width, width, 1) for x in outputs]

    dm = (d_out.astype(F32) * valid).astype(BF)
    e1, products, _ = mlp_backward(dm, gains1[1], mlp1, saved_m1, 4, 1)
    local1 = mlp_sums(products)

    both = []
    for output, stat in zip(outputs, statistics):
        high = stat.astype(BF)
        rest = (stat - high.astype(F32)).astype(BF)
        parts = jnp.concatenate([high, rest], axis=0).reshape(-1, width)
        parts = jnp.pad(parts, ((0, -parts.shape[0] % 16), (0, 0)))
        both.append(jnp.concatenate([output + e1[:1, :1] * 0, parts], axis=0))
    kept = jnp.where(section == 0, both[0], both[1])
    sent = jnp.where(section == 0, both[1], both[0])

    d_qkv, products, _ = attention_backward(e1, attn1, low, tables, saved_a1, 1, 9)
    local1.append(shard_sum(products))
    crosses = [(sent, 2), (local1[0], 1)]
    grad1, home1, (sent, down1) = attention_end(
        d_qkv, e1, attn1, gains1[0], saved_a1, 5, 1, (products,), crosses
    )
    by_section = jnp.stack([jnp.where(section == 0, kept, sent), jnp.where(section == 0, sent, kept)])
    everything = lax.all_gather(by_section, "gx", axis=0)
    owner = jnp.sum(jnp.where(dealing == shard, jnp.arange(shards), 0))
    halves = lax.dynamic_slice(
        everything, ((owner // 2) * 2, owner % 2, 0, 0), (2, 1) + everything.shape[2:]
    )[:, 0]
    layer_out = join_halves(halves[0, :half], halves[1, :half])
    stat_rows = 4 * half // width
    parts = halves[:, half : half + stat_rows].astype(F32).reshape(2, 4, half)
    stat_halves = parts[:, :2] + parts[:, 2:]
    stats_out = join_halves(stat_halves[0].T, stat_halves[1].T).T

    dm = (grad1.astype(F32) * valid).astype(BF)
    crosses = [(local1[1], 1), (local1[2], 1)]
    e1, products, (gate1, up1) = mlp_backward(dm, gains0[1], mlp0, saved_m0, 6, 0, crosses)
    local0 = mlp_sums(products)
    d_qkv, products, (down0,) = attention_backward(
        e1, attn0, low, tables, saved_a0, 0, 11, local0[:1]
    )
    local0.append(shard_sum(products))
    crosses = [(local1[3], 1), (local0[1], 0)]
    grad0, home0, (attn_sum1, gate0) = attention_end(
        d_qkv, e1, attn0, gains0[0], saved_a0, 7, 0, (products, everything), crosses
    )

    input_grads = [lax.dynamic_slice_in_dim(x, column * width, width, 1) for x in (grad0, grad1)]
    local0[2] = local0[2] + grad0[:1, :1] * 0
    received0 = [down0, gate0] + crossing([(x, 0) for x in local0[2:]])
    received1 = [down1, gate1, up1, attn_sum1]
    totals = [
        jnp.where(section == 0, a0.astype(F32) + r0.astype(F32), a1.astype(F32) + r1.astype(F32))
        for a0, r0, a1, r1 in zip(local0, received0, local1, received1)
    ]
    s_down, s_gate, s_up, s_attn = totals
    s_out = s_attn[:, low:]
    q_width = w_query.shape[2]

    attn_sum = jnp.sum(s_attn[:, :low] * attn_own[:block_rows, :low].astype(F32), axis=1)
    mlp_sum = jnp.sum(s_gate * w_gate[0].astype(F32) + s_up * w_up[0].astype(F32), axis=1)
    sums = jnp.stack([attn_sum, mlp_sum]).reshape(-1, 2 * HD)
    sum_rows = sums.shape[0]
    sums = jnp.pad(sums, ((0, -sum_rows % 16), (0, 0)))
    spread = jnp.concatenate([s_attn[:, q_width:low], sums], axis=0).astype(BF)
    spread = lax.all_gather(spread, "gy", axis=0).astype(F32)
    gains = jnp.sum(spread[:, block_rows : block_rows + sum_rows], axis=0).reshape(2, block_rows)
    gains = gains / both_gains.astype(F32)
    kv_sum = spread[:, :block_rows].reshape(KVH, -1, block_rows, 2, HD).sum(axis=1)
    kv_sum = kv_sum.transpose(2, 1, 0, 3).reshape(2, block_rows, KVH * HD)

    kept = jnp.where(section == 0, input_grads[0], input_grads[1])
    sent = jnp.where(section == 0, home0, home1)
    keep = jnp.where(core == section, kept, sent)
    give = swap_pairs(jnp.where(core == section, sent, kept), "gx")
    back_home = join_halves(jnp.where(core == 0, keep, give), jnp.where(core == 0, give, keep))
    return (
        layer_out[None],
        stats_out[None],
        back_home[None],
        gains[None, 0],
        s_attn[None, :, :q_width],
        kv_sum[None, 0],
        kv_sum[None, 1],
        s_out.T[None],
        gains[None, 1],
        s_gate[None],
        s_up[None],
        s_down.T[None],
    )


def solution(mesh):
    rows_cols = P("section", "gx", "gy")
    cols_rows = P("section", "gy", "gx")
    rows_only = P("section", "gx", None)
    gain = P("section", "gx")
    return jax.shard_map(
        on_device,
        mesh=mesh,
        in_specs=(
            P("gx", "gy"), P("gx", "gy"), P(), P(), gain, rows_cols, rows_only, rows_only,
            cols_rows, gain, rows_cols, rows_cols, cols_rows,
        ),
        out_specs=(
            rows_cols, P("section", None, "gx"), rows_cols, gain, rows_cols, rows_only, rows_only,
            cols_rows, gain, rows_cols, rows_cols, cols_rows,
        ),
        check_vma=False,
    )
```

profile of v0, /device:TPU:0, one launch (start us, length us, event | category | flops | bytes accessed | tf_op | source)
XLA Modules:
  0.0 960.2 jit_solution(1359876195221452879)
XLA Ops:
  15.9 2.9 collective-permute-start.1
  20.2 41.0 %line_gather.2.h_ref.resid_ref = bf16[512,2048]{1,0:T(8,128)(2,1)} custom-call(bf16[512,512]{1,0:T(8,128)(2,1)} %slice.210.mine_ref), custom_call_target="tpu_custom_call" | custom-call | bytes 150000000 | tf_op jit(solution)/shard_map/line_gather/pallas_call | solution.py:151
  64.7 33.8 %collective-permute-done.2.rest_10_.rest_2_.rest_6_ = bf16[512,1408]{1,0:T(8,128)(2,1)S(1)} collective-permute-done((bf16[512,1408]{1,0:T(8,128)(2,1)}, bf16[512,1408]{1,0:T(8,128)(2,1)S(1)}, u32[]{:S(2)}, u32[]{:S(2)}) %collective-permute-start.2) | collective-permute-done | bytes 1441824 | tf_op jit(solution)/shard_map/ppermute | solution.py:32
  111.6 17.4 %attend_whole.2 = (bf16[512,512]{1,0:T(8,128)(2,1)}, bf16[512,2048]{1,0:T(8,128)(2,1)}, f32[512,1]{1,0:T(8,128)}, bf16[512,512]{1,0:T(8,128)(2,1)}, f32[8,512]{1...) custom-call(bf16[512,2048]{1,0:T(8,128)(2,1)} %line_gather.2.h_ref.resid_ref, ...), custom_call_target="tpu_custom_call" | custom-call | flops 4294967296 | bytes 70000000 | tf_op jit(solution)/shard_map/attend_whole/pallas_call | solution.py:455
  131.7 38.8 %line_gather.3.rest_3_ = bf16[512,2048]{1,0:T(8,128)(2,1)} custom-call(bf16[512,512]{1,0:T(8,128)(2,1)} %slice_add_fusion.mine_ref), custom_call_target="tpu_custom_call" | custom-call | bytes 150000000 | tf_op jit(solution)/shard_map/line_gather/pallas_call | solution.py:151
  170.5 3.3 multiply_convert_fusion.1.resid_ref
  176.3 63.9 %line_out.2 = (bf16[512,2048]{1,0:T(8,128)(2,1)}, bf16[4,512,1408]{2,1,0:T(8,128)(2,1)}, bf16[4,1408,512]{2,1,0:T(8,128)(2,1)}) custom-call(f32[1,2048]{1,0:T(1,128)} %broadcast_4_gain_ref.2.gain_ref, bf16[512,2048]{1,0:T(8,128)(2,1)} %line_gather.2.h_ref.resid_ref, f32[512,1]{1,0:T(8,128)} %broadcast_7_valid_ref.2.valid_ref, ...), custom_call_target="tpu_custom_call" | custom-call | flops 1073741824 | bytes 209715200 | tf_op jit(solution)/shard_map/line_out/pallas_call | solution.py:1063
  240.2 70.5 %line_mlp.2 = (bf16[512,2048]{1,0:T(8,128)(2,1)}, bf16[512,2048]{1,0:T(8,128)(2,1)}, f32[512,1]{1,0:T(8,128)}, bf16[512,1408]{1,0:T(8,128)(2,1)}, bf16[512,1408]...) custom-call(f32[1,2048]{1,0:T(1,128)} %bitcast.151, ...), custom_call_target="tpu_custom_call" | custom-call | flops 8858370048 | bytes 209715200 | tf_op jit(solution)/shard_map/line_mlp/pallas_call | solution.py:1063
  312.8 16.7 %attend_whole.3 = (bf16[512,512]{1,0:T(8,128)(2,1)}, bf16[512,2048]{1,0:T(8,128)(2,1)}, f32[512,1]{1,0:T(8,128)}, bf16[512,512]{1,0:T(8,128)(2,1)}, f32[8,512]{1...) custom-call(bf16[512,2048]{1,0:T(8,128)(2,1)} %get-tuple-element.74.h_ref.resid_ref, ...), custom_call_target="tpu_custom_call" | custom-call | flops 4294967296 | bytes 70000000 | tf_op jit(solution)/shard_map/attend_whole/pallas_call | solution.py:455
  329.5 66.7 %line_out.3 = (bf16[512,2048]{1,0:T(8,128)(2,1)}, bf16[4,512,1408]{2,1,0:T(8,128)(2,1)}, bf16[4,1408,512]{2,1,0:T(8,128)(2,1)}) custom-call(f32[1,2048]{1,0:T(1,128)} %broadcast_4_gain_ref.2.gain_ref, bf16[512,2048]{1,0:T(8,128)(2,1)} %get-tuple-element.74.h_ref.resid_ref, f32[512,1]{1,0:T(8,128)} %broadcast_7_valid_ref.2.valid_ref, ...), custom_call_target="tpu_custom_call" | custom-call | flops 1073741824 | bytes 209715200 | tf_op jit(solution)/shard_map/line_out/pallas_call | solution.py:1063
  396.3 69.6 %line_mlp.3 = (bf16[512,2048]{1,0:T(8,128)(2,1)}, bf16[512,2048]{1,0:T(8,128)(2,1)}, f32[512,1]{1,0:T(8,128)}, bf16[512,1408]{1,0:T(8,128)(2,1)}, bf16[512,1408]{1,0:T(8,128)(2,1)}, /*index=5*/bf16[512,1408]{1,0:T(8,128)(2,1)}) custom-call(f32[1,2048]{1,0:T(1,128)} %bitcast.155, bf16[512,2048]{1,0:T(8,128)(2,1)} %get-tuple-element.77.resid_ref.h_ref, ...), custom_call_target="tpu_custom_call" | custom-call | flops 8858370048 | bytes 209715200 | tf_op jit(solution)/shard_map/line_mlp/pallas_call | solution.py:1063
  465.9 75.6 %line_mlp_back.2 = (bf16[512,2048]{1,0:T(8,128)(2,1)}, bf16[1,512,1408]{2,1,0:T(8,128)(2,1)}, bf16[2,512,1408]{2,1,0:T(8,128)(2,1)}, bf16[2,512,1408]{2,1,0:T(8,128)(2,1)}, bf16[512,1408]{1,0:T(8,128)(2,1)}) custom-call(f32[1,2048]{1,0:T(1,128)} %bitcast.156, bf16[512,2048]{1,0:T(8,128)(2,1)} %multiply_convert_fusion.1.resid_ref, ...), custom_call_target="tpu_custom_call" | custom-call | flops 8858370048 | bytes 209715200 | tf_op jit(solution)/shard_map/line_mlp_back/pallas_call | solution.py:1063
  550.5 22.5 %attend_whole_back.2.rest_0_ = bf16[512,640]{1,0:T(8,128)(2,1)} custom-call(bf16[512,2048]{1,0:T(8,128)(2,1)} %get-tuple-element.86.e1_ref.resid_ref, bf16[512,512]{1,0:T(8,128)(2,1)} %get-tuple-element.91.rot_ref, f32[8,512]{1,0:T(8,128)} %get-tuple-element.92.lse_ref, bf16[1024,64]{1,0:T(8,128)(2,1)} %get-tuple-element.93.k_ref, ...), custom_call_target="tpu_custom_call" | custom-call | flops 10737418240 | bytes 90000000 | tf_op jit(solution)/shard_map/attend_whole_back/pallas_call | solution.py:490
  573.0 3.1 convolution_convert_fusion.1
  580.2 65.0 %line_back.2 = (bf16[512,2048]{1,0:T(8,128)(2,1)}, bf16[528,512]{1,0:T(8,128)(2,1)}, bf16[512,1408]{1,0:T(8,128)(2,1)}, bf16[512,512]{1,0:T(8,128)(2,1)}) custom-call(f32[1,2048]{1,0:T(1,128)} %bitcast.154, bf16[512,2048]{1,0:T(8,128)(2,1)} %get-tuple-element.86.e1_ref.resid_ref, f32[512,1]{1,0:T(8,128)} %broadcast_7_valid_ref.2.valid_ref, ...), custom_call_target="tpu_custom_call" | custom-call | flops 1342177280 | bytes 209715200 | tf_op jit(solution)/shard_map/line_back/pallas_call | solution.py:1063
  650.9 88.5 %line_mlp_back.3 = (bf16[512,2048]{1,0:T(8,128)(2,1)}, bf16[1,512,1408]{2,1,0:T(8,128)(2,1)}, bf16[2,512,1408]{2,1,0:T(8,128)(2,1)}, bf16[2,512,1408]{2,1,0:T(8,...) custom-call(f32[1,2048]{1,0:T(1,128)} %bitcast.152, ...), custom_call_target="tpu_custom_call" | custom-call | flops 8858370048 | bytes 209715200 | tf_op jit(solution)/shard_map/line_mlp_back/pallas_call | solution.py:1063
  744.4 38.6 %attend_whole_back.3 = (bf16[512,640]{1,0:T(8,128)(2,1)}, bf16[512,1408]{1,0:T(8,128)(2,1)}) custom-call(bf16[512,2048]{1,0:T(8,128)(2,1)} %get-tuple-element.107.e1_ref.resid_ref, bf16[512,512]{1,0:T(8,128)(2,1)} %get-tuple-element.108.rot_ref, f32[8,512]{1,0:T(8,128)} %get-tuple-element.109.lse_ref, bf16[1024,64]{1,0:T(8,128)(2,1)} %get-tuple-element.110.k_ref, ...), custom_call_target="tpu_custom_call" | custom-call | flops 10737418240 | bytes 90000000 | tf_op jit(solution)/shard_map/attend_whole_back/pallas_call | solution.py:490
  792.5 4.0 select_bitcast_fusion
  796.5 3.4 copy.113
  801.3 65.7 %line_back.3 = (bf16[512,2048]{1,0:T(8,128)(2,1)}, bf16[512,1152]{1,0:T(8,128)(2,1)}, bf16[512,1408]{1,0:T(8,128)(2,1)}, bf16[512,512]{1,0:T(8,128)(2,1)}) custom-call(f32[1,2048]{1,0:T(1,128)} %bitcast.150, bf16[512,2048]{1,0:T(8,128)(2,1)} %get-tuple-element.107.e1_ref.resid_ref, f32[512,1]{1,0:T(8,128)} %broadcast_7_valid_ref.2.valid_ref, ...), custom_call_target="tpu_custom_call" | custom-call | flops 1342177280 | bytes 209715200 | tf_op jit(solution)/shard_map/line_back/pallas_call | solution.py:1063
  883.8 24.6 %collective-permute-done.7 = bf16[512,1408]{1,0:T(8,128)(2,1)} collective-permute-done((bf16[512,1408]{1,0:T(8,128)(2,1)}, bf16[512,1408]{1,0:T(8,128)(2,1)}, u32[]{:S(2)}, u32[]{:S(2)}) %collective-permute-start.7) | collective-permute-done | bytes 1441824 | tf_op jit(solution)/shard_map/ppermute | solution.py:1186
  908.3 8.9 fusion.4
  917.3 13.0 %collective-permute-done.6 = bf16[512,1152]{1,0:T(8,128)(2,1)S(1)} collective-permute-done((bf16[512,1152]{1,0:T(8,128)(2,1)}, bf16[512,1152]{1,0:T(8,128)(2,1)S(1)}, u32[]{:S(2)}, u32[]{:S(2)}) %collective-permute-start.6) | collective-permute-done | bytes 1179680 | tf_op jit(solution)/shard_map/ppermute | solution.py:1186
  933.0 15.7 %all_gather.28 = bf16[4,528,128]{2,1,0:T(8,128)(2,1)S(1)} all-gather(bf16[1,528,128]{2,1,0:T(8,128)(2,1)S(1)} %pad_maximum_fusion.7), channel_id=1, replica_groups=mesh['section'=2,'gx'=4,'gy'=4] {'gy'}, dimensions={0}, use_global_device_ids=true | all-gather | bytes 675840 | tf_op jit(solution)/shard_map/all_gather | solution.py:1374
  (243 shorter events, 85.9 us)
Async XLA Ops:
  7.2 103.0 %all-gather.7.cloned.1.call-start = ((), (), s32[]{:S(2)}) async-start(), calls=%async_computation.12 | async-start | bytes 6266880 | tf_op jit(solution)/shard_map/all_gather | solution.py:61
  10.2 3.1 collective-permute-start
  15.9 47.1 %collective-permute-start.1 = (bf16[544,1152]{1,0:T(8,128)(2,1)S(1)}, bf16[544,1152]{1,0:T(8,128)(2,1)S(1)}, u32[]{:S(2)}, u32[]{:S(2)}) collective-permute-start(bf16[544,1152]{1,0:T(8,128)(2,1)S(1)} %pad_maximum_fusion.2.rest_7_.rest_1_.rest_2_), channel_id=1, source_target_pairs={{0,16},{16,0},{1,17},{17,1},{2,18},{18,2},{3,19},{19,3},{4,20},{20... | collective-permute-start | bytes 3760136 | tf_op jit(solution)/shard_map/ppermute | solution.py:32
  19.3 43.7 %copy-start.12 = (bf16[512,1024]{1,0:T(8,128)(2,1)}, bf16[512,1024]{1,0:T(8,128)(2,1)S(1)}, u32[]{:S(2)}) copy-start(bf16[512,1024]{1,0:T(8,128)(2,1)S(1)} %maximum_select_fusion) | copy-start | bytes 3145732
  19.3 43.7 %copy-start.8 = (bf16[512,1152]{1,0:T(8,128)(2,1)S(1)}, bf16[512,1152]{1,0:T(8,128)(2,1)}, u32[]{:S(2)}) copy-start(bf16[512,1152]{1,0:T(8,128)(2,1)} %copy-done.7) | copy-start | bytes 3538948
  19.3 43.7 %copy-start.35 = (bf16[32,1152]{1,0:T(8,128)(2,1)S(1)}, bf16[32,1152]{1,0:T(8,128)(2,1)}, u32[]{:S(2)}) copy-start(bf16[32,1152]{1,0:T(8,128)(2,1)} %copy-done.34) | copy-start | bytes 221188
  64.6 109.3 %all-gather.9.cloned.1.call-start = ((), (), s32[]{:S(2)}) async-start(), calls=%async_computation.13 | async-start | bytes 7208960 | tf_op jit(solution)/shard_map/all_gather | solution.py:61
  64.6 37.8 %copy-start = (bf16[1,512,1408]{2,1,0:T(8,128)(2,1)S(1)}, bf16[1,512,1408]{2,1,0:T(8,128)(2,1)}, u32[]{:S(2)}) copy-start(bf16[1,512,1408]{2,1,0:T(8,128)(2,1)} %param.24) | copy-start | bytes 4325380
  64.6 38.2 %copy-start.2 = (bf16[1,1408,512]{2,1,0:T(8,128)(2,1)S(1)}, bf16[1,1408,512]{2,1,0:T(8,128)(2,1)}, u32[]{:S(2)}) copy-start(bf16[1,1408,512]{2,1,0:T(8,128)(2,1)} %param.25) | copy-start | bytes 4325380
  64.6 41.2 %copy-start.46 = (s32[4]{0:T(128)S(1)}, s32[4]{0:T(128)}, u32[]{:S(2)}) copy-start(s32[4]{0:T(128)} %param.15) | copy-start | bytes 52
  64.6 33.9 %collective-permute-start.2 = (bf16[512,1408]{1,0:T(8,128)(2,1)}, bf16[512,1408]{1,0:T(8,128)(2,1)S(1)}, u32[]{:S(2)}, u32[]{:S(2)}) collective-permute-start(bf16[512,1408]{1,0:T(8,128)(2,1)} %bitcast.133), channel_id=1, source_target_pairs={{0,16},{16,0},{1,17},{17,1},{2,18},{18,2},{3,19},{19,3},{4,20},{20... | collective-permute-start | bytes 4325384 | tf_op jit(solution)/shard_map/ppermute | solution.py:32
  102.3 548.6 %reduce-scatter.7.cloned.1.call-start = ((), (), s32[]{:S(2)}) async-start(), calls=%async_computation.6 | async-start | bytes 4325376 | tf_op jit(solution)/shard_map/reduce_scatter | solution.py:95
  102.4 71.4 %collective-permute-start.3 = (bf16[512,1408]{1,0:T(8,128)(2,1)S(1)}, bf16[512,1408]{1,0:T(8,128)(2,1)}, u32[]{:S(2)}, u32[]{:S(2)}) collective-permute-start(bf16[512,1408]{1,0:T(8,128)(2,1)S(1)} %bitcast.117), channel_id=1, source_target_pairs={{0,16},{16,0},{1,17},{17,1},{2,18},{18,2},{3,19},{19,3},{4,20},{20... | collective-permute-start | bytes 4325384 | tf_op jit(solution)/shard_map/ppermute | solution.py:32
  102.8 71.0 %collective-permute-start.4 = (bf16[1408,512]{1,0:T(8,128)(2,1)S(1)}, bf16[1408,512]{1,0:T(8,128)(2,1)}, u32[]{:S(2)}, u32[]{:S(2)}) collective-permute-start(bf16[1408,512]{1,0:T(8,128)(2,1)S(1)} %bitcast.127), channel_id=1, source_target_pairs={{0,16},{16,0},{1,17},{17,1},{2,18},{18,2},{3,19},{19,3},{4,20},{20... | collective-permute-start | bytes 4325384 | tf_op jit(solution)/shard_map/ppermute | solution.py:32
  541.5 109.4 %reduce-scatter.9.cloned.1.call-start = ((), (), s32[]{:S(2)}) async-start(), calls=%async_computation.7 | async-start | bytes 4325376 | tf_op jit(solution)/shard_map/reduce_scatter | solution.py:95
  542.1 257.8 %all-gather.11.cloned.1.call-start = ((), (), s32[]{:S(2)}) async-start(), calls=%async_computation.14 | async-start | bytes 5406720 | tf_op jit(solution)/shard_map/all_gather | solution.py:1332
  647.6 153.7 %reduce-scatter.11.cloned.1.call-start = ((), (), s32[]{:S(2)}) async-start(), calls=%async_computation.8 | async-start | bytes 5898240 | tf_op jit(solution)/shard_map/reduce_scatter | solution.py:90
  648.2 153.1 %reduce-scatter.13.cloned.1.call-start = ((), (), s32[]{:S(2)}) async-start(), calls=%async_computation.9 | async-start | bytes 4325376 | tf_op jit(solution)/shard_map/reduce_scatter | solution.py:95
  739.5 129.5 %reduce-scatter.17.cloned.1.call-start = ((), (), s32[]{:S(2)}) async-start(), calls=%async_computation.11 | async-start | bytes 4325376 | tf_op jit(solution)/shard_map/reduce_scatter | solution.py:95
  740.2 139.9 %reduce-scatter.15.cloned.1.call-start = ((), (), s32[]{:S(2)}) async-start(), calls=%async_computation.10 | async-start | bytes 5898240 | tf_op jit(solution)/shard_map/reduce_scatter | solution.py:90
  744.4 38.6 %copy-start.48 = (bf16[512,2048]{1,0:T(8,128)(2,1)S(1)}, bf16[512,2048]{1,0:T(8,128)(2,1)}, u32[]{:S(2)}) copy-start(bf16[512,2048]{1,0:T(8,128)(2,1)} %get-tuple-element.116) | copy-start | bytes 6291460
  871.6 36.7 %collective-permute-start.7 = (bf16[512,1408]{1,0:T(8,128)(2,1)}, bf16[512,1408]{1,0:T(8,128)(2,1)}, u32[]{:S(2)}, u32[]{:S(2)}) collective-permute-start(bf16[512,1408]{1,0:T(8,128)(2,1)} %broadcast_add_fusion), channel_id=1, source_target_pairs={{16,0},{17,1},{18,2},{19,3},{20,4},{21,5},{22,6},{23,7},{24,8},{25... | collective-permute-start | bytes 4325384 | tf_op jit(solution)/shard_map/ppermute | solution.py:1186
  874.5 2.0 collective-permute-start.5
  880.1 50.2 %collective-permute-start.6 = (bf16[512,1152]{1,0:T(8,128)(2,1)}, bf16[512,1152]{1,0:T(8,128)(2,1)S(1)}, u32[]{:S(2)}, u32[]{:S(2)}) collective-permute-start(bf16[512,1152]{1,0:T(8,128)(2,1)} %reduce-scatter.15.cloned.1.call-done), channel_id=1, source_target_pairs={{16,0},{17,1},{18,2},{19,3},{20,4},{21,5},{22,6},{23,7},{24,8},{25... | collective-permute-start | bytes 3538952 | tf_op jit(solution)/shard_map/ppermute | solution.py:1186
  (43 other events, 257.0 us)
Sparse Core Ops, SparseCore 0:
  64.7 38.3 all-gather.6
  105.2 43.3 all-gather.8
  541.6 39.0 reduce-scatter.6
  582.9 40.4 reduce-scatter.8
  647.7 35.6 all-gather.10
  685.8 59.5 reduce-scatter.10
  747.8 38.9 reduce-scatter.12
  789.0 40.4 reduce-scatter.16
  832.3 47.8 reduce-scatter.14
where the time goes:
time: 969 us; the launch traced here: 960 us
  Pallas kernels  740 us (76%)
  waiting for transfers between devices  77.3 us (8%)
  other arithmetic  54 us (6%)
  local copies, waits for them, and re-layouts  33.2 us (3%)
  between operations  21 us (2%)
  blocking collectives  15.7 us (2%)
    pallas_call x8, Pallas kernels, line_sum(): pl.pallas_call(functools.partial(line_kernel, kind, valid is not None, lo...  565 us
    pallas_call x2, Pallas kernels, line_gather(): pl.pallas_call(line_gather_kernel, out_shape=jax.ShapeDtypeStruct((rows,...  79.8 us
    pallas_call x2, Pallas kernels, attend_whole_back(): pl.pallas_call(functools.partial(attend_whole_back_kernel, w_layer, len(w...  61.1 us
    ppermute x2, waiting for transfers between devices, crossing(): return [lax.ppermute(x, 'section', pairs[way]) for x, way in crosses]  37.6 us
    ppermute x6, waiting for transfers between devices, swap_pairs(): return lax.ppermute(values, axis, [(i, i ^ by) for i in range(count)])  35 us
    pallas_call x2, Pallas kernels, attend_whole(): pl.pallas_call(functools.partial(attend_whole_kernel, w_layer, len(w_list...  34.1 us
  transfers between devices with their start and end apart: 17, of which 6 were waited for; matrix products, arithmetic and copies ran while one was open for 8% of the time, Pallas kernels for 39%

commit v1 on v0

--- a/solution.py
+++ b/solution.py
@@ -1344,17 +1344,19 @@
     crosses = [(local1[1], 1), (local1[2], 1)]
     e1, products, (gate1, up1) = mlp_backward(dm, gains0[1], mlp0, saved_m0, 6, 0, crosses)
     local0 = mlp_sums(products)
-    d_qkv, products, (down0,) = attention_backward(
-        e1, attn0, low, tables, saved_a0, 0, 11, local0[:1]
+    middle = local0[0].shape[0] // 2
+    d_qkv, products, (down_low,) = attention_backward(
+        e1, attn0, low, tables, saved_a0, 0, 11, [local0[0][:middle]]
     )
     local0.append(shard_sum(products))
-    crosses = [(local1[3], 1), (local0[1], 0)]
-    grad0, home0, (attn_sum1, gate0) = attention_end(
+    crosses = [(local1[3], 1), (local0[1], 0), (local0[0][middle:], 0)]
+    grad0, home0, (attn_sum1, gate0, down_high) = attention_end(
         d_qkv, e1, attn0, gains0[0], saved_a0, 7, 0, (products, everything), crosses
     )
 
     input_grads = [lax.dynamic_slice_in_dim(x, column * width, width, 1) for x in (grad0, grad1)]
     local0[2] = local0[2] + grad0[:1, :1] * 0
+    down0 = jnp.concatenate([down_low, down_high], axis=0)
     received0 = [down0, gate0] + crossing([(x, 0) for x in local0[2:]])
     received1 = [down1, gate1, up1, attn_sum1]
     totals = [

time: 969 us -> 957 us (0.988)
  Pallas kernels: 740 us -> 728 us
    pallas_call x2, Pallas kernels: 61.1 us -> 46 us  [attend_whole_back(): pl.pallas_call(functools.partial(attend_whole_back_kernel, w_layer, len(w...]
    ppermute x2, waiting for transfers between devices: 37.6 us -> 26.9 us  [crossing(): return [lax.ppermute(x, 'section', pairs[way]) for x, way in crosses]]
where the time goes in v1:
time: 957 us; the launch traced here: 949 us
  Pallas kernels  728 us (76%)
  waiting for transfers between devices  78.5 us (8%)
  other arithmetic  52.1 us (5%)
  local copies, waits for them, and re-layouts  33.3 us (3%)
  between operations  21.3 us (2%)
  blocking collectives  14.9 us (2%)
  matrix products  11.3 us (1%)
    pallas_call x8, Pallas kernels, line_sum(): pl.pallas_call(functools.partial(line_kernel, kind, valid is not None, lo...  568 us
    pallas_call x2, Pallas kernels, line_gather(): pl.pallas_call(line_gather_kernel, out_shape=jax.ShapeDtypeStruct((rows,...  79.8 us
    pallas_call x2, Pallas kernels, attend_whole_back(): pl.pallas_call(functools.partial(attend_whole_back_kernel, w_layer, len(w...  46 us
    ppermute x6, waiting for transfers between devices, swap_pairs(): return lax.ppermute(values, axis, [(i, i ^ by) for i in range(count)])  34.8 us
    pallas_call x2, Pallas kernels, attend_whole(): pl.pallas_call(functools.partial(attend_whole_kernel, w_layer, len(w_list...  34.1 us
    ppermute x2, waiting for transfers between devices, crossing(): return [lax.ppermute(x, 'section', pairs[way]) for x, way in crosses]  26.9 us
  transfers between devices with their start and end apart: 17, of which 6 were waited for; matrix products, arithmetic and copies ran while one was open for 8% of the time, Pallas kernels for 39%

profile of v1, /device:TPU:0, one launch (start us, length us, event | category | flops | bytes accessed | tf_op | source)
XLA Modules:
  0.0 949.0 jit_solution(9620205905963274516)
XLA Ops:
  20.2 41.0 %line_gather.2.h_ref.resid_ref = bf16[512,2048]{1,0:T(8,128)(2,1)} custom-call(bf16[512,512]{1,0:T(8,128)(2,1)} %slice.218.mine_ref), custom_call_target="tpu_custom_call" | custom-call | bytes 150000000 | tf_op jit(solution)/shard_map/line_gather/pallas_call | solution.py:151
  64.7 33.8 %collective-permute-done.2.rest_10_.rest_2_.rest_6_ = bf16[512,1408]{1,0:T(8,128)(2,1)S(1)} collective-permute-done((bf16[512,1408]{1,0:T(8,128)(2,1)}, bf16[512,1408]{1,0:T(8,128)(2,1)S(1)}, u32[]{:S(2)}, u32[]{:S(2)}) %collective-permute-start.2) | collective-permute-done | bytes 1441824 | tf_op jit(solution)/shard_map/ppermute | solution.py:32
  111.6 17.4 %attend_whole.2 = (bf16[512,512]{1,0:T(8,128)(2,1)}, bf16[512,2048]{1,0:T(8,128)(2,1)}, f32[512,1]{1,0:T(8,128)}, bf16[512,512]{1,0:T(8,128)(2,1)}, f32[8,512]{1...) custom-call(bf16[512,2048]{1,0:T(8,128)(2,1)} %line_gather.2.h_ref.resid_ref, ...), custom_call_target="tpu_custom_call" | custom-call | flops 4294967296 | bytes 70000000 | tf_op jit(solution)/shard_map/attend_whole/pallas_call | solution.py:455
  131.7 38.8 %line_gather.3.rest_3_ = bf16[512,2048]{1,0:T(8,128)(2,1)} custom-call(bf16[512,512]{1,0:T(8,128)(2,1)} %slice_add_fusion.mine_ref), custom_call_target="tpu_custom_call" | custom-call | bytes 150000000 | tf_op jit(solution)/shard_map/line_gather/pallas_call | solution.py:151
  170.5 3.3 multiply_convert_fusion.1.resid_ref
  176.3 63.8 %line_out.2 = (bf16[512,2048]{1,0:T(8,128)(2,1)}, bf16[4,512,1408]{2,1,0:T(8,128)(2,1)}, bf16[4,1408,512]{2,1,0:T(8,128)(2,1)}) custom-call(f32[1,2048]{1,0:T(1,128)} %broadcast_4_gain_ref.2.gain_ref, bf16[512,2048]{1,0:T(8,128)(2,1)} %line_gather.2.h_ref.resid_ref, f32[512,1]{1,0:T(8,128)} %broadcast_7_valid_ref.2.valid_ref, ...), custom_call_target="tpu_custom_call" | custom-call | flops 1073741824 | bytes 209715200 | tf_op jit(solution)/shard_map/line_out/pallas_call | solution.py:1063
  240.1 70.1 %line_mlp.2 = (bf16[512,2048]{1,0:T(8,128)(2,1)}, bf16[512,2048]{1,0:T(8,128)(2,1)}, f32[512,1]{1,0:T(8,128)}, bf16[512,1408]{1,0:T(8,128)(2,1)}, bf16[512,1408]...) custom-call(f32[1,2048]{1,0:T(1,128)} %bitcast.151, ...), custom_call_target="tpu_custom_call" | custom-call | flops 8858370048 | bytes 209715200 | tf_op jit(solution)/shard_map/line_mlp/pallas_call | solution.py:1063
  312.4 16.7 %attend_whole.3 = (bf16[512,512]{1,0:T(8,128)(2,1)}, bf16[512,2048]{1,0:T(8,128)(2,1)}, f32[512,1]{1,0:T(8,128)}, bf16[512,512]{1,0:T(8,128)(2,1)}, f32[8,512]{1...) custom-call(bf16[512,2048]{1,0:T(8,128)(2,1)} %get-tuple-element.75.h_ref.resid_ref, ...), custom_call_target="tpu_custom_call" | custom-call | flops 4294967296 | bytes 70000000 | tf_op jit(solution)/shard_map/attend_whole/pallas_call | solution.py:455
  329.1 67.1 %line_out.3 = (bf16[512,2048]{1,0:T(8,128)(2,1)}, bf16[4,512,1408]{2,1,0:T(8,128)(2,1)}, bf16[4,1408,512]{2,1,0:T(8,128)(2,1)}) custom-call(f32[1,2048]{1,0:T(1,128)} %broadcast_4_gain_ref.2.gain_ref, bf16[512,2048]{1,0:T(8,128)(2,1)} %get-tuple-element.75.h_ref.resid_ref, f32[512,1]{1,0:T(8,128)} %broadcast_7_valid_ref.2.valid_ref, ...), custom_call_target="tpu_custom_call" | custom-call | flops 1073741824 | bytes 209715200 | tf_op jit(solution)/shard_map/line_out/pallas_call | solution.py:1063
  396.1 69.6 %line_mlp.3 = (bf16[512,2048]{1,0:T(8,128)(2,1)}, bf16[512,2048]{1,0:T(8,128)(2,1)}, f32[512,1]{1,0:T(8,128)}, bf16[512,1408]{1,0:T(8,128)(2,1)}, bf16[512,1408]{1,0:T(8,128)(2,1)}, /*index=5*/bf16[512,1408]{1,0:T(8,128)(2,1)}) custom-call(f32[1,2048]{1,0:T(1,128)} %bitcast.155, bf16[512,2048]{1,0:T(8,128)(2,1)} %get-tuple-element.78.resid_ref.h_ref, ...), custom_call_target="tpu_custom_call" | custom-call | flops 8858370048 | bytes 209715200 | tf_op jit(solution)/shard_map/line_mlp/pallas_call | solution.py:1063
  465.7 75.5 %line_mlp_back.2 = (bf16[512,2048]{1,0:T(8,128)(2,1)}, bf16[1,512,1408]{2,1,0:T(8,128)(2,1)}, bf16[2,512,1408]{2,1,0:T(8,128)(2,1)}, bf16[2,512,1408]{2,1,0:T(8,128)(2,1)}, bf16[512,1408]{1,0:T(8,128)(2,1)}) custom-call(f32[1,2048]{1,0:T(1,128)} %bitcast.156, bf16[512,2048]{1,0:T(8,128)(2,1)} %multiply_convert_fusion.1.resid_ref, ...), custom_call_target="tpu_custom_call" | custom-call | flops 8858370048 | bytes 209715200 | tf_op jit(solution)/shard_map/line_mlp_back/pallas_call | solution.py:1063
  550.3 22.5 %attend_whole_back.2.rest_0_ = bf16[512,640]{1,0:T(8,128)(2,1)} custom-call(bf16[512,2048]{1,0:T(8,128)(2,1)} %get-tuple-element.87.e1_ref.resid_ref, bf16[512,512]{1,0:T(8,128)(2,1)} %get-tuple-element.92.rot_ref, f32[8,512]{1,0:T(8,128)} %get-tuple-element.93.lse_ref, bf16[1024,64]{1,0:T(8,128)(2,1)} %get-tuple-element.94.k_ref, ...), custom_call_target="tpu_custom_call" | custom-call | flops 10737418240 | bytes 90000000 | tf_op jit(solution)/shard_map/attend_whole_back/pallas_call | solution.py:490
  572.8 3.1 convolution_convert_fusion.1
  580.0 64.9 %line_back.2 = (bf16[512,2048]{1,0:T(8,128)(2,1)}, bf16[528,512]{1,0:T(8,128)(2,1)}, bf16[512,1408]{1,0:T(8,128)(2,1)}, bf16[512,512]{1,0:T(8,128)(2,1)}) custom-call(f32[1,2048]{1,0:T(1,128)} %bitcast.154, bf16[512,2048]{1,0:T(8,128)(2,1)} %get-tuple-element.87.e1_ref.resid_ref, f32[512,1]{1,0:T(8,128)} %broadcast_7_valid_ref.2.valid_ref, ...), custom_call_target="tpu_custom_call" | custom-call | flops 1342177280 | bytes 209715200 | tf_op jit(solution)/shard_map/line_back/pallas_call | solution.py:1063
  650.7 88.6 %line_mlp_back.3 = (bf16[512,2048]{1,0:T(8,128)(2,1)}, bf16[1,512,1408]{2,1,0:T(8,128)(2,1)}, bf16[2,512,1408]{2,1,0:T(8,128)(2,1)}, bf16[2,512,1408]{2,1,0:T(8,...) custom-call(f32[1,2048]{1,0:T(1,128)} %bitcast.152, ...), custom_call_target="tpu_custom_call" | custom-call | flops 8858370048 | bytes 209715200 | tf_op jit(solution)/shard_map/line_mlp_back/pallas_call | solution.py:1063
  745.0 23.5 %attend_whole_back.3 = (bf16[512,640]{1,0:T(8,128)(2,1)}, bf16[256,1408]{1,0:T(8,128)(2,1)}) custom-call(bf16[512,2048]{1,0:T(8,128)(2,1)} %get-tuple-element.108.e1_ref.resid_ref, bf16[512,512]{1,0:T(8,128)(2,1)} %get-tuple-element.109.rot_ref, f32[8,512]{1,0:T(8,128)} %get-tuple-element.110.lse_ref, bf16[1024,64]{1,0:T(8,128)(2,1)} %get-tuple-element.111.k_ref, ...), custom_call_target="tpu_custom_call" | custom-call | flops 10737418240 | bytes 90000000 | tf_op jit(solution)/shard_map/attend_whole_back/pallas_call | solution.py:490
  781.1 5.7 reduce-scatter.13.cloned.1.call-done.rest_5_
  786.8 68.8 %line_back.3 = (bf16[512,2048]{1,0:T(8,128)(2,1)}, bf16[512,1152]{1,0:T(8,128)(2,1)}, bf16[512,1408]{1,0:T(8,128)(2,1)}, bf16[256,1408]{1,0:T(8,128)(2,1)}, bf16[512,512]{1,0:T(8,128)(2,1)}) custom-call(f32[1,2048]{1,0:T(1,128)} %bitcast.150, bf16[512,2048]{1,0:T(8,128)(2,1)} %get-tuple-element.108.e1_ref.resid_ref, ...), custom_call_target="tpu_custom_call" | custom-call | flops 1342177280 | bytes 209715200 | tf_op jit(solution)/shard_map/line_back/pallas_call | solution.py:1063
  866.6 3.5 copy.113
  871.0 9.2 reduce-scatter.15.cloned.1.call-done
  883.8 13.5 %collective-permute-done.7 = bf16[512,1408]{1,0:T(8,128)(2,1)} collective-permute-done((bf16[512,1408]{1,0:T(8,128)(2,1)}, bf16[512,1408]{1,0:T(8,128)(2,1)}, u32[]{:S(2)}, u32[]{:S(2)}) %collective-permute-start.7) | collective-permute-done | bytes 1441824 | tf_op jit(solution)/shard_map/ppermute | solution.py:1186
  897.3 8.9 fusion.4
  906.3 13.5 %collective-permute-done.6 = bf16[512,1152]{1,0:T(8,128)(2,1)S(1)} collective-permute-done((bf16[512,1152]{1,0:T(8,128)(2,1)}, bf16[512,1152]{1,0:T(8,128)(2,1)S(1)}, u32[]{:S(2)}, u32[]{:S(2)}) %collective-permute-start.6) | collective-permute-done | bytes 1179680 | tf_op jit(solution)/shard_map/ppermute | solution.py:1186
  922.5 14.9 %all_gather.28 = bf16[4,528,128]{2,1,0:T(8,128)(2,1)S(1)} all-gather(bf16[1,528,128]{2,1,0:T(8,128)(2,1)S(1)} %pad_maximum_fusion.7), channel_id=1, replica_groups=mesh['section'=2,'gx'=4,'gy'=4] {'gy'}, dimensions={0}, use_global_device_ids=true | all-gather | bytes 675840 | tf_op jit(solution)/shard_map/all_gather | solution.py:1376
  (250 shorter events, 90.0 us)
Async XLA Ops:
  7.2 103.0 %all-gather.7.cloned.1.call-start = ((), (), s32[]{:S(2)}) async-start(), calls=%async_computation.12 | async-start | bytes 6266880 | tf_op jit(solution)/shard_map/all_gather | solution.py:61
  10.2 3.1 collective-permute-start
  15.9 47.0 %collective-permute-start.1 = (bf16[544,1152]{1,0:T(8,128)(2,1)S(1)}, bf16[544,1152]{1,0:T(8,128)(2,1)S(1)}, u32[]{:S(2)}, u32[]{:S(2)}) collective-permute-start(bf16[544,1152]{1,0:T(8,128)(2,1)S(1)} %pad_maximum_fusion.2.rest_7_.rest_1_.rest_2_), channel_id=1, source_target_pairs={{0,16},{16,0},{1,17},{17,1},{2,18},{18,2},{3,19},{19,3},{4,20},{20... | collective-permute-start | bytes 3760136 | tf_op jit(solution)/shard_map/ppermute | solution.py:32
  19.3 43.7 %copy-start.11 = (bf16[512,1024]{1,0:T(8,128)(2,1)}, bf16[512,1024]{1,0:T(8,128)(2,1)S(1)}, u32[]{:S(2)}) copy-start(bf16[512,1024]{1,0:T(8,128)(2,1)S(1)} %maximum_select_fusion) | copy-start | bytes 3145732
  19.3 43.7 %copy-start.8 = (bf16[512,1152]{1,0:T(8,128)(2,1)S(1)}, bf16[512,1152]{1,0:T(8,128)(2,1)}, u32[]{:S(2)}) copy-start(bf16[512,1152]{1,0:T(8,128)(2,1)} %copy-done.7) | copy-start | bytes 3538948
  19.3 43.7 %copy-start.38 = (bf16[32,1152]{1,0:T(8,128)(2,1)S(1)}, bf16[32,1152]{1,0:T(8,128)(2,1)}, u32[]{:S(2)}) copy-start(bf16[32,1152]{1,0:T(8,128)(2,1)} %copy-done.37) | copy-start | bytes 221188
  64.5 109.3 %all-gather.9.cloned.1.call-start = ((), (), s32[]{:S(2)}) async-start(), calls=%async_computation.13 | async-start | bytes 7208960 | tf_op jit(solution)/shard_map/all_gather | solution.py:61
  64.6 37.8 %copy-start = (bf16[1,512,1408]{2,1,0:T(8,128)(2,1)S(1)}, bf16[1,512,1408]{2,1,0:T(8,128)(2,1)}, u32[]{:S(2)}) copy-start(bf16[1,512,1408]{2,1,0:T(8,128)(2,1)} %param.24) | copy-start | bytes 4325380
  64.6 38.2 %copy-start.2 = (bf16[1,1408,512]{2,1,0:T(8,128)(2,1)S(1)}, bf16[1,1408,512]{2,1,0:T(8,128)(2,1)}, u32[]{:S(2)}) copy-start(bf16[1,1408,512]{2,1,0:T(8,128)(2,1)} %param.25) | copy-start | bytes 4325380
  64.6 41.2 %copy-start.49 = (s32[4]{0:T(128)S(1)}, s32[4]{0:T(128)}, u32[]{:S(2)}) copy-start(s32[4]{0:T(128)} %param.15) | copy-start | bytes 52
  64.6 33.9 %collective-permute-start.2 = (bf16[512,1408]{1,0:T(8,128)(2,1)}, bf16[512,1408]{1,0:T(8,128)(2,1)S(1)}, u32[]{:S(2)}, u32[]{:S(2)}) collective-permute-start(bf16[512,1408]{1,0:T(8,128)(2,1)} %bitcast.133), channel_id=1, source_target_pairs={{0,16},{16,0},{1,17},{17,1},{2,18},{18,2},{3,19},{19,3},{4,20},{20... | collective-permute-start | bytes 4325384 | tf_op jit(solution)/shard_map/ppermute | solution.py:32
  102.3 548.4 %reduce-scatter.7.cloned.1.call-start = ((), (), s32[]{:S(2)}) async-start(), calls=%async_computation.6 | async-start | bytes 4325376 | tf_op jit(solution)/shard_map/reduce_scatter | solution.py:95
  102.4 71.4 %collective-permute-start.3 = (bf16[512,1408]{1,0:T(8,128)(2,1)S(1)}, bf16[512,1408]{1,0:T(8,128)(2,1)}, u32[]{:S(2)}, u32[]{:S(2)}) collective-permute-start(bf16[512,1408]{1,0:T(8,128)(2,1)S(1)} %bitcast.117), channel_id=1, source_target_pairs={{0,16},{16,0},{1,17},{17,1},{2,18},{18,2},{3,19},{19,3},{4,20},{20... | collective-permute-start | bytes 4325384 | tf_op jit(solution)/shard_map/ppermute | solution.py:32
  102.8 71.0 %collective-permute-start.4 = (bf16[1408,512]{1,0:T(8,128)(2,1)S(1)}, bf16[1408,512]{1,0:T(8,128)(2,1)}, u32[]{:S(2)}, u32[]{:S(2)}) collective-permute-start(bf16[1408,512]{1,0:T(8,128)(2,1)S(1)} %bitcast.127), channel_id=1, source_target_pairs={{0,16},{16,0},{1,17},{17,1},{2,18},{18,2},{3,19},{19,3},{4,20},{20... | collective-permute-start | bytes 4325384 | tf_op jit(solution)/shard_map/ppermute | solution.py:32
  541.3 109.3 %reduce-scatter.9.cloned.1.call-start = ((), (), s32[]{:S(2)}) async-start(), calls=%async_computation.7 | async-start | bytes 4325376 | tf_op jit(solution)/shard_map/reduce_scatter | solution.py:95
  541.9 236.1 %all-gather.11.cloned.1.call-start = ((), (), s32[]{:S(2)}) async-start(), calls=%async_computation.14 | async-start | bytes 5406720 | tf_op jit(solution)/shard_map/all_gather | solution.py:1332
  647.4 133.8 %reduce-scatter.11.cloned.1.call-start = ((), (), s32[]{:S(2)}) async-start(), calls=%async_computation.8 | async-start | bytes 5898240 | tf_op jit(solution)/shard_map/reduce_scatter | solution.py:90
  647.9 138.9 %reduce-scatter.13.cloned.1.call-start = ((), (), s32[]{:S(2)}) async-start(), calls=%async_computation.9 | async-start | bytes 4325376 | tf_op jit(solution)/shard_map/reduce_scatter | solution.py:95
  739.3 118.2 %reduce-scatter.17.cloned.1.call-start = ((), (), s32[]{:S(2)}) async-start(), calls=%async_computation.11 | async-start | bytes 4325376 | tf_op jit(solution)/shard_map/reduce_scatter | solution.py:95
  740.1 140.1 %reduce-scatter.15.cloned.1.call-start = ((), (), s32[]{:S(2)}) async-start(), calls=%async_computation.10 | async-start | bytes 5898240 | tf_op jit(solution)/shard_map/reduce_scatter | solution.py:90
  860.3 37.0 %collective-permute-start.7 = (bf16[512,1408]{1,0:T(8,128)(2,1)}, bf16[512,1408]{1,0:T(8,128)(2,1)}, u32[]{:S(2)}, u32[]{:S(2)}) collective-permute-start(bf16[512,1408]{1,0:T(8,128)(2,1)} %broadcast_add_fusion), channel_id=1, source_target_pairs={{16,0},{17,1},{18,2},{19,3},{20,4},{21,5},{22,6},{23,7},{24,8},{25... | collective-permute-start | bytes 4325384 | tf_op jit(solution)/shard_map/ppermute | solution.py:1186
  864.3 5.8 collective-permute-start.5
  871.0 26.3 %copy-start.3 = (bf16[1,512,1408]{2,1,0:T(8,128)(2,1)S(1)}, bf16[1,512,1408]{2,1,0:T(8,128)(2,1)}, u32[]{:S(2)}) copy-start(bf16[1,512,1408]{2,1,0:T(8,128)(2,1)} %param.23) | copy-start | bytes 4325380
  880.2 39.6 %collective-permute-start.6 = (bf16[512,1152]{1,0:T(8,128)(2,1)}, bf16[512,1152]{1,0:T(8,128)(2,1)S(1)}, u32[]{:S(2)}, u32[]{:S(2)}) collective-permute-start(bf16[512,1152]{1,0:T(8,128)(2,1)} %reduce-scatter.15.cloned.1.call-done), channel_id=1, source_target_pairs={{16,0},{17,1},{18,2},{19,3},{20,4},{21,5},{22,6},{23,7},{24,8},{25... | collective-permute-start | bytes 3538952 | tf_op jit(solution)/shard_map/ppermute | solution.py:1186
  (46 other events, 262.0 us)
Sparse Core Ops, SparseCore 0:
  64.6 38.3 all-gather.6
  105.1 43.3 all-gather.8
  541.4 39.0 reduce-scatter.6
  582.7 40.4 reduce-scatter.8
  647.5 35.8 all-gather.10
  685.7 59.5 reduce-scatter.10
  747.6 39.1 reduce-scatter.12
  789.1 40.4 reduce-scatter.16
  832.3 47.8 reduce-scatter.14
